TPU v7x, 256 devices: a whole 4x4x8 slice. The times are simulated.
256 devices in a mesh: recv: 32 (over x, z_lo, core), win: 8 (over y, z_hi).
Axes of the slice: x: 4, y: 4, z: 8 (z_hi: 2, z_lo: 4; z = z_hi * 4 + z_lo), core: 2. Of those that a mesh axis runs over, the one named last changes fastest.
Arguments:
- records: bfloat16 [512, 8, 2048], P('recv', 'win'), may hold values from -60 to 60, as said below
- usable: int32 [512, 8], P('recv', 'win'), may hold values from 0 to 1
- sources: int32 [128], replicated, may hold values from 0 to 511, as said below
Outputs:
- correlations: bfloat16 [128, 512, 512], P('win', 'recv')
Inputs may be any that keep to these rules, and one draw needn't show every extreme that they name: Each entry of records is a finite sample. `sources`: 128 distinct channel indices.
All inputs are finite; a program needn't handle non-finite values.
Results may differ from a plain program's by a relative error of at most 0.0064.
Values may be sent and summed in bfloat16 or wider, within the bound.
No kernel may reach another device: no remote copies, remote signals or barrier semaphores. Data moves between devices by JAX's collectives and lax.ppermute only.
A program may use at most 64 MiB of HBM per device.

v0:
```python
import math

import jax
import jax.numpy as jnp
from jax import lax
from jax.sharding import PartitionSpec as P

HALF = 256
SMOOTH = 32


def forward_table(length):
    bin_count = length // 2
    sample_ids = lax.broadcasted_iota(jnp.int32, (length, bin_count), 0)
    bin_ids = lax.broadcasted_iota(jnp.int32, (length, bin_count), 1)
    phases = (sample_ids * bin_ids % length).astype(jnp.float32) * (2.0 * math.pi / length)
    return jnp.concatenate([jnp.cos(phases), -jnp.sin(phases)], axis=1).astype(jnp.bfloat16)


def band_matrix(bin_count, reach):
    row_ids = lax.broadcasted_iota(jnp.int32, (bin_count, bin_count), 0)
    col_ids = lax.broadcasted_iota(jnp.int32, (bin_count, bin_count), 1)
    inside = (jnp.abs(row_ids - col_ids) <= reach).astype(jnp.float32)
    return inside / jnp.sum(inside, axis=0, keepdims=True)


def inverse_table(length, lag_half):
    bin_count = length // 2
    bin_ids = lax.broadcasted_iota(jnp.int32, (bin_count, 2 * lag_half), 0)
    lag_ids = lax.broadcasted_iota(jnp.int32, (bin_count, 2 * lag_half), 1) - lag_half
    phases = (bin_ids * lag_ids % length).astype(jnp.float32) * (2.0 * math.pi / length)
    factor = jnp.where(bin_ids == 0, 1.0, 2.0).astype(jnp.float32) / math.sqrt(length)
    return jnp.concatenate([factor * jnp.cos(phases), -factor * jnp.sin(phases)], axis=0)


def whiten(flat_rows, dft_table, band_mean):
    widened = flat_rows.astype(jnp.float32)
    centred = (widened - jnp.mean(widened, axis=-1, keepdims=True)).astype(jnp.bfloat16)
    spectrum = jnp.dot(centred, dft_table, preferred_element_type=jnp.float32)
    bin_half = spectrum.shape[-1] // 2
    real_part = spectrum[:, :bin_half]
    imag_part = spectrum[:, bin_half:]
    amplitude = jnp.sqrt(real_part * real_part + imag_part * imag_part)
    smooth = jnp.dot(amplitude, band_mean, precision=lax.Precision.HIGHEST)
    return spectrum / (jnp.concatenate([smooth, smooth], axis=1) + 1e-06)


def cross_term(src_block, src_weight, rec_spec, rec_weight):
    highest = lax.Precision.HIGHEST
    bin_half = src_block.shape[-1] // 2
    left_side = src_block * src_weight[:, :, None]
    right_side = rec_spec * rec_weight[:, :, None]
    left_re = left_side[..., :bin_half]
    left_im = left_side[..., bin_half:]
    right_re = right_side[..., :bin_half]
    right_im = right_side[..., bin_half:]
    real_part = jnp.einsum("nwf,cwf->ncf", left_re, right_re, precision=highest) + jnp.einsum(
        "nwf,cwf->ncf", left_im, right_im, precision=highest
    )
    imag_part = jnp.einsum("nwf,cwf->ncf", left_im, right_re, precision=highest) - jnp.einsum(
        "nwf,cwf->ncf", left_re, right_im, precision=highest
    )
    return jnp.concatenate([real_part, imag_part], axis=-1)


def local(records, usable, sources):
    highest = lax.Precision.HIGHEST
    ch_dev, win_dev, length = records.shape
    source_total = sources.shape[0]
    dft_table = forward_table(length)
    band_mean = band_matrix(length // 2, SMOOTH)
    inverse = inverse_table(length, HALF)
    channel_ids = lax.axis_index("recv") * ch_dev + lax.broadcasted_iota(jnp.int32, (1, ch_dev), 1)
    onehot = sources[:, None] == channel_ids
    rec_weight = usable.astype(jnp.float32)
    rec_spec = whiten(records.reshape(ch_dev * win_dev, length), dft_table, band_mean).reshape(
        ch_dev, win_dev, length
    )
    local_mask = jnp.dot(onehot.astype(jnp.float32), rec_weight, precision=highest)
    picked = jnp.einsum("sc,cwf->swf", onehot.astype(jnp.float32), rec_spec, precision=highest)
    source_spec, src_weight = lax.psum((picked, local_mask), "recv")
    all_rec, all_src = (
        lax.all_gather(rec_weight, "win", axis=1, tiled=True),
        lax.all_gather(src_weight, "win", axis=1, tiled=True),
    )
    pair_count = jnp.dot(all_src, all_rec.T, precision=highest)
    own_rows = source_total // lax.axis_size("win")
    owner_first = lax.axis_index("win") * own_rows
    stacked = lax.psum_scatter(
        jnp.dot(
            cross_term(source_spec, src_weight, rec_spec, rec_weight), inverse, precision=highest
        ),
        "win",
        scatter_dimension=0,
        tiled=True,
    )
    own_counts = lax.dynamic_slice_in_dim(pair_count, owner_first, own_rows, 0)
    return (stacked / jnp.sqrt(jnp.maximum(own_counts, 1.0))[:, :, None]).astype(jnp.bfloat16)


def solution(mesh):
    in_specs = (P("recv", "win", None), P("recv", "win"), P())
    out_specs = P("win", "recv", None)
    return jax.shard_map(local, mesh=mesh, in_specs=in_specs, out_specs=out_specs, check_vma=False)
```

profile of v0, /device:TPU:1, one launch (start us, length us, event | category | flops | bytes accessed | tf_op | source)
XLA Modules:
  0.0 497.5 jit_solution(6085416622412403599)
XLA Ops:
  6.5 0.0 copy-start.1
  6.5 0.0 all-reduce.2.cloned.1.call-start
  6.5 34.9 %negate_convert_fusion = (bf16[2048,1024]{1,0:T(8,128)(2,1)}, bf16[2048,1024]{1,0:T(8,128)(2,1)}) fusion(), kind=kLoop, calls=%fused_computation.16 | loop fusion | flops 35651584 | bytes 8388608 | tf_op jit(solution)/shard_map/convert.1
  41.5 0.2 convert_reduce_fusion
  41.7 0.0 copy-done.1
  41.7 0.1 convert_reduce_fusion.1
  41.8 4.2 fusion.7
  46.0 0.0 copy-start.2
  46.0 0.0 copy-start.3
  46.0 1.8 fusion.16
  47.9 0.0 copy-done.2
  47.9 1.6 convolution_bitcast_fusion
  49.5 0.0 all-reduce.2.cloned.1.call-update
  49.5 0.0 reduce-scatter.2.cloned.1.call-start
  49.5 0.0 copy-done.3
  49.5 0.2 convolution_bitcast_fusion.1
  49.8 70.0 %psum.15 = f32[128,1]{0,1:T(1,128)S(1)} all-reduce(f32[128,1]{0,1:T(1,128)S(1)} %convolution_bitcast_fusion.1), channel_id=1, replica_groups=mesh['recv'=32,'win'=8] {'recv'}, use_global_device_ids=true, to_apply=%region_3.4 | all-reduce | flops 128 | bytes 1024 | tf_op jit(solution)/shard_map/psum | solution.py:81
  119.8 0.1 multiply_bitcast_fusion
  119.9 9.4 %cosine_multiply_fusion = (f32[1024,512]{1,0:T(8,128)S(1)}, f32[1024,512]{1,0:T(8,128)}) fusion(s32[512]{0:T(512)S(1)} %iota_add_fusion, f32[1024]{0:T(1024)S(1)} %get-tuple-element.17, f32[1024]{0:T(1024)S(1)} %get-tuple-element.18), kind=kLoop, calls=%fused_computation.36 | loop fusion | flops 8388608 | bytes 4204544 | tf_op jit(solution)/shard_map/mul | solution.py:33
  129.3 202.4 %all-reduce.2.cloned.1.call-done = f32[128,1,2048]{2,0,1:T(8,128)} async-done(((f32[128,1,2048]{2,0,1:T(8,128)}), f32[128,1,2048]{2,0,1:T(8,128)}) %all-reduce.2.cloned.1.call-update) | async-done | bytes 1048592 | tf_op jit(solution)/shard_map/psum | solution.py:81
  331.7 1.4 broadcast_multiply_fusion
  333.1 0.1 slice_bitcast_fusion.1
  333.2 0.0 copy-start
  333.2 2.5 add_bitcast_fusion
  335.7 0.0 copy-done
  335.7 28.0 %fusion = f32[128,16,512]{2,0,1:T(8,128)} fusion(f32[128,16,1024]{2,0,1:T(8,128)S(1)} %get-tuple-element.6, f32[128,16,1024]{2,0,1:T(8,128)S(1)} %get-tuple-element.5, f32[1024,512]{1,0:T(8,128)S(1)} %copy-done, f32[1024,512]{1,0:T(8,128)S(1)} %get-tuple-element.11), kind=kOutput, calls=%fused_computation | convolution fusion | flops 25775046656 | bytes 25165824 | tf_op jit(solution)/shard_map/dot_general | solution.py:90
  363.6 0.0 reduce-scatter.2.cloned.1.call-update
  363.7 25.4 %all-gather.1 = f32[8,1,16]{2,1,0:T(1,128)S(1)} all-gather(f32[1,1,16]{2,1,0:T(1,128)S(1)} %get-tuple-element.13), channel_id=1, replica_groups=mesh['recv'=32,'win'=8] {'win'}, dimensions={0}, use_global_device_ids=true | all-gather | bytes 576 | tf_op jit(solution)/shard_map/all_gather | solution.py:83
  389.1 19.4 %all-gather = f32[8,1,128]{2,1,0:T(1,128)S(1)} all-gather(f32[1,1,128]{2,1,0:T(1,128)S(1)} %bitcast.50), channel_id=1, replica_groups=mesh['recv'=32,'win'=8] {'win'}, dimensions={0}, use_global_device_ids=true | all-gather | bytes 4608 | tf_op jit(solution)/shard_map/all_gather | solution.py:84
  408.5 0.3 fusion.45
  408.8 0.1 copy.8
  408.9 79.7 %reduce-scatter.2.cloned.1.call-done = f32[16,16,512]{2,0,1:T(8,128)} async-done(((f32[128,16,512]{2,0,1:T(8,128)}), f32[16,16,512]{2,0,1:T(8,128)}) %reduce-scatter.2.cloned.1.call-update) | async-done | bytes 524304 | tf_op jit(solution)/shard_map/reduce_scatter | solution.py:89
  488.6 1.1 divide_convert_fusion
  489.8 0.9 copy.9
  (7 shorter events, 0.1 us)
Async XLA Ops:
  6.5 35.1 %copy-start.1 = (bf16[16,1,2048]{2,0,1:T(8,128)(2,1)S(1)}, bf16[16,1,2048]{2,0,1:T(8,128)(2,1)}, u32[]{:S(2)}) copy-start(bf16[16,1,2048]{2,0,1:T(8,128)(2,1)} %param.3) | copy-start | bytes 196612
  6.5 325.2 %all-reduce.2.cloned.1.call-start = ((), (), s32[]{:S(2)}) async-start(), calls=%async_computation.1 | async-start | bytes 2097152 | tf_op jit(solution)/shard_map/psum | solution.py:81
  46.0 1.8 copy-start.2
  46.0 3.5 copy-start.3
  49.5 439.1 %reduce-scatter.2.cloned.1.call-start = ((), (), s32[]{:S(2)}) async-start(), calls=%async_computation.2 | async-start | bytes 4718592 | tf_op jit(solution)/shard_map/reduce_scatter | solution.py:89
  333.2 2.5 copy-start
Sparse Core Ops, SparseCore 0:
  49.6 282.0 all-reduce.1
  363.8 124.7 reduce-scatter.1
where the time goes:
time: 498 us; the launch traced here: 497 us
  waiting for transfers between devices  282 us (57%)
  blocking collectives  115 us (23%)
  other arithmetic  49.8 us (10%)
  matrix products  36 us (7%)
  between operations  13.5 us (3%)
    psum x1, waiting for transfers between devices, local(): source_spec, src_weight = lax.psum((picked, local_mask), 'recv')  202 us
    reduce_scatter x1, waiting for transfers between devices, local(): lax.psum_scatter(jnp.dot(cross_term(source_spec, src_weight, rec_spec, re...  79.7 us
    psum x1, blocking collectives, local(): source_spec, src_weight = lax.psum((picked, local_mask), 'recv')  70 us
    another operation x1, other arithmetic  34.9 us
    dot_general x1, matrix products, local(): jnp.dot(cross_term(source_spec, src_weight, rec_spec, rec_weight), invers...  28 us
    all_gather x1, blocking collectives, local(): lax.all_gather(rec_weight, 'win', axis=1, tiled=True)  25.4 us
    all_gather x1, blocking collectives, local(): lax.all_gather(src_weight, 'win', axis=1, tiled=True)  19.4 us
  transfers between devices with their start and end apart: 2, of which 2 were waited for; matrix products, arithmetic and copies ran while one was open for 2% of the time, Pallas kernels for 0%

commit v1 on v0

v1 whole, which is shorter than its diff:
```python
import functools
import math

import jax
import jax.numpy as jnp
import numpy as np
from jax import lax
from jax.experimental import pallas as pl
from jax.experimental.pallas import tpu as pltpu
from jax.sharding import Mesh
from jax.sharding import PartitionSpec as P

LENGTH = 2048
BINS = LENGTH // 2
HALF = 256
LAGS = 2 * HALF
SMOOTH = 32
LANES = 128
SLICES = LENGTH // LANES
BLOCKS = BINS // LANES
WINS = 8
OWN = 16
SOURCES = 128
CHANNELS = 512
MARK = 1e30
MARK_LIMIT = 1e29
BF16 = jnp.bfloat16
F32 = jnp.float32


def forward_table():
    samples = np.arange(LENGTH)[:, None]
    bins = np.arange(BINS)[None, :]
    phases = (samples * bins % LENGTH).astype(np.float32) * np.float32(2.0 * math.pi / LENGTH)
    table = np.stack([np.cos(phases), -np.sin(phases)], axis=1).reshape(LENGTH, 2, BLOCKS, LANES)
    return table.transpose(2, 0, 1, 3).reshape(BLOCKS, LENGTH, 2 * LANES).astype(jnp.bfloat16)


def inverse_table():
    bins = np.arange(BINS)[:, None]
    lags = np.arange(LAGS)[None, :] - HALF
    phases = (bins * lags % LENGTH).astype(np.float32) * np.float32(2.0 * math.pi / LENGTH)
    factor = np.where(bins == 0, 1.0, 2.0).astype(np.float32) / np.float32(math.sqrt(LENGTH))
    table = np.stack([factor * np.cos(phases), -factor * np.sin(phases)], axis=0)
    table = table.reshape(2, BLOCKS, LANES, LAGS).transpose(1, 0, 2, 3)
    return table.reshape(LENGTH, LAGS).astype(jnp.bfloat16)


def band_table():
    rows = np.arange(3 * LANES)[:, None] - LANES
    cols = np.arange(LANES)[None, :]
    return (np.abs(rows - cols) <= SMOOTH).astype(np.float32).astype(jnp.bfloat16)


def band_share():
    bins = np.arange(BINS)
    count = np.minimum(bins, SMOOTH) + np.minimum(BINS - 1 - bins, SMOOTH) + 1
    share = (1.0 / count).astype(np.float32).reshape(BLOCKS, 1, LANES)
    return np.broadcast_to(share, (BLOCKS, 8, LANES)).copy()


def centre_kernel(records_ref, usable_ref, slices_ref, rows_ref):
    widened = records_ref[...].astype(F32)
    mean = jnp.sum(widened, axis=1, keepdims=True) * (1.0 / LENGTH)
    centred = widened - mean
    row_ids = lax.broadcasted_iota(jnp.int32, (OWN, OWN), 0)
    col_ids = lax.broadcasted_iota(jnp.int32, (OWN, OWN), 1)
    flags = jnp.broadcast_to(usable_ref[...].astype(F32), (OWN, OWN))
    flag = jnp.sum(jnp.where(row_ids == col_ids, flags, 0.0), axis=1, keepdims=True)
    marked = jnp.where(flag > 0.5, centred, MARK).astype(BF16)
    rows_ref[...] = marked
    for part in range(SLICES):
        piece = marked[:, part * LANES : (part + 1) * LANES]
        slices_ref[2 * part] = piece
        slices_ref[2 * part + 1] = piece


def pick_kernel(sources_ref, all_ref, picked_ref):
    core = lax.axis_index("core")
    rows = all_ref[...].reshape(CHANNELS, LANES)
    channel_ids = lax.broadcasted_iota(jnp.int32, (CHANNELS, SOURCES), 0)
    onehot = (channel_ids == sources_ref[...]).astype(F32).astype(BF16)
    picked = lax.dot_general(
        onehot, rows, (((0,), (0,)), ((), ())), preferred_element_type=F32
    ).reshape(WINS, 2, 8, LANES)
    half = jnp.where(core == 0, picked[:, 0], picked[:, 1]).astype(BF16)
    for place in range(SLICES):
        picked_ref[pl.ds(place * WINS, WINS)] = half


def unmark(values):
    return jnp.where(values.astype(F32) > MARK_LIMIT, 0.0, values.astype(F32)).astype(BF16)


def correlate_kernel(
    own_ref, other_ref, rec_ref, table_ref, band_ref, share_ref, inverse_ref, out_ref,
    rows, spec, amp, cross,
):
    core = lax.axis_index("core")
    side = lax.axis_index("zh")
    for part in range(SLICES):
        lanes = pl.ds(part * LANES, LANES)
        rows[0:64, lanes] = unmark(own_ref[part].reshape(64, LANES))
        rows[64:128, lanes] = unmark(other_ref[part].reshape(64, LANES))
    rec_flags = []
    for win in range(WINS):
        slot = (win // 2) * 2 + (win % 2 + side) % 2
        received = rec_ref[slot]
        rows[pl.ds(128 + win * OWN, OWN), :] = unmark(received)
        rec_flags.append((received[:, :LANES].astype(F32) < MARK_LIMIT).astype(F32))

    for block in range(BLOCKS):
        part = jnp.dot(rows[...], table_ref[block], preferred_element_type=F32)
        spec[block] = part
        real, imag = part[:, :LANES], part[:, LANES:]
        amp[:, pl.ds(block * LANES, LANES)] = jnp.sqrt(real * real + imag * imag).astype(BF16)

    for block in range(BLOCKS):
        first, last = max(block - 1, 0), min(block + 2, BLOCKS)
        offset = (first - block + 1) * LANES
        width = (last - first) * LANES
        total = jnp.dot(
            amp[:, pl.ds(first * LANES, width)],
            band_ref[pl.ds(offset, width), :],
            preferred_element_type=F32,
        )
        scale = 1.0 / (total * share_ref[block, 0:1, :] + 1e-6)
        spec[block, :, :LANES] = spec[block, :, :LANES] * scale
        spec[block, :, LANES:] = spec[block, :, LANES:] * scale

    def one_block(block, carry):
        rec_re = [spec[block, pl.ds(128 + w * OWN, OWN), :LANES] for w in range(WINS)]
        rec_im = [spec[block, pl.ds(128 + w * OWN, OWN), LANES:] for w in range(WINS)]
        for index in range(OWN):
            base = (index // 8) * 64 + index % 8
            real = imag = None
            for w in range(WINS):
                row = base + w * 8
                src_re = jnp.broadcast_to(spec[block, row : row + 1, :LANES], (OWN, LANES))
                src_im = jnp.broadcast_to(spec[block, row : row + 1, LANES:], (OWN, LANES))
                re_part = src_re * rec_re[w] + src_im * rec_im[w]
                im_part = src_im * rec_re[w] - src_re * rec_im[w]
                real = re_part if real is None else real + re_part
                imag = im_part if imag is None else imag + im_part
            cross[block, pl.ds(index * OWN, OWN), :LANES] = real.astype(BF16)
            cross[block, pl.ds(index * OWN, OWN), LANES:] = imag.astype(BF16)
        return carry

    lax.fori_loop(0, BLOCKS, one_block, 0)

    lagged = jnp.dot(cross[0], inverse_ref[0 : 2 * LANES, :], preferred_element_type=F32)
    for block in range(1, BLOCKS):
        lagged += jnp.dot(
            cross[block], inverse_ref[pl.ds(block * 2 * LANES, 2 * LANES), :], preferred_element_type=F32
        )
    for which, ref in enumerate((own_ref, other_ref)):
        half = jnp.where(which == 0, core, 1 - core) * 8
        flags = (ref[0].astype(F32) < MARK_LIMIT).astype(F32)
        for index in range(8):
            count = jnp.zeros((OWN, LANES), F32)
            for w in range(WINS):
                count += jnp.broadcast_to(flags[w, index : index + 1, :], (OWN, LANES)) * rec_flags[w]
            scale = lax.rsqrt(jnp.maximum(count, 1.0))
            pair = (which * 8 + index) * OWN
            for piece in range(LAGS // LANES):
                lanes = slice(piece * LANES, (piece + 1) * LANES)
                out_ref[half + index, :, lanes] = (lagged[pair : pair + OWN, lanes] * scale).astype(BF16)


def local(records, usable, sources):
    rows_in = records.reshape(OWN, LENGTH)
    slices, rows = pl.pallas_call(
        centre_kernel,
        out_shape=(
            jax.ShapeDtypeStruct((2 * SLICES, OWN, LANES), BF16),
            jax.ShapeDtypeStruct((OWN, LENGTH), BF16),
        ),
    )(rows_in, usable.reshape(1, OWN))
    all_channels = lax.all_to_all(slices, ("x", "z", "core"), 0, 0)
    opposite = lax.ppermute(rows, "zh", [(0, 1), (1, 0)])
    received = lax.all_gather(jnp.concatenate([rows, opposite], axis=0), "y", axis=0)
    picked = pl.pallas_call(
        pick_kernel,
        out_shape=jax.ShapeDtypeStruct((SLICES * WINS, 8, LANES), BF16),
    )(sources.reshape(1, SOURCES), all_channels)
    own = lax.all_to_all(picked, ("x", "z", "y", "zh"), 0, 0)
    other = lax.ppermute(own, "core", [(0, 1), (1, 0)])
    own = own.reshape(SLICES, WINS, 8, LANES)
    other = other.reshape(SLICES, WINS, 8, LANES)
    return pl.pallas_call(
        correlate_kernel,
        out_shape=jax.ShapeDtypeStruct((OWN, OWN, LAGS), BF16),
        scratch_shapes=[
            pltpu.VMEM((256, LENGTH), BF16),
            pltpu.VMEM((BLOCKS, 256, 2 * LANES), F32),
            pltpu.VMEM((256, BINS), BF16),
            pltpu.VMEM((BLOCKS, 256, 2 * LANES), BF16),
        ],
        compiler_params=pltpu.CompilerParams(vmem_limit_bytes=40 * 2**20),
    )(
        own,
        other,
        received.reshape(WINS, OWN, LENGTH),
        jnp.asarray(forward_table()),
        jnp.asarray(band_table()),
        jnp.asarray(band_share()),
        jnp.asarray(inverse_table()),
    )


def solution(mesh):
    split = Mesh(mesh.devices.reshape(4, 4, 2, 4, 2), ("x", "z", "core", "y", "zh"))
    recv, win = ("x", "z", "core"), ("y", "zh")
    in_specs = (P(recv, win, None), P(recv, win), P())
    out_specs = P(win, recv, None)
    return jax.shard_map(local, mesh=split, in_specs=in_specs, out_specs=out_specs, check_vma=False)
```

time: 498 us -> 75.9 us (0.15)
  waiting for transfers between devices: 282 us -> 7.61 us
  blocking collectives: 115 us -> 29.3 us
  other arithmetic: 49.8 us -> 0.85 us
  matrix products: 36 us -> 0 us
  starting transfers between devices: 0.04 us -> 20.4 us
  between operations: 13.5 us -> 0.02 us
  Pallas kernels: 0 us -> 9.85 us
  local copies, waits for them, and re-layouts: 1.05 us -> 6.64 us
    psum x1 -> x0, waiting for transfers between devices: 202 us -> none  [local(): source_spec, src_weight = lax.psum((picked, local_mask), 'recv')]
    reduce_scatter x1 -> x0, waiting for transfers between devices: 79.7 us -> none  [local(): lax.psum_scatter(jnp.dot(cross_term(source_spec, src_weight, rec_spec, re...]
    psum x1 -> x0, blocking collectives: 70 us -> none  [local(): source_spec, src_weight = lax.psum((picked, local_mask), 'recv')]
    dot_general x6 -> x0, matrix products: 36 us -> none  [the longest x1 28 us: local(): jnp.dot(cross_term(source_spec, src_weight, rec_spec, rec_weight), invers...]
    another operation x1 -> x0, other arithmetic: 34.9 us -> none
    all_gather x2 -> x1, blocking collectives: 44.8 us -> 10.5 us  [local(): lax.all_gather(jnp.concatenate([rows, opposite], axis=0), 'y', axis=0)]
    all_to_all x0 -> x1, blocking collectives: none -> 18.8 us  [local(): all_channels = lax.all_to_all(slices, ('x', 'z', 'core'), 0, 0)]
    mul x3 -> x0, other arithmetic: 10.8 us -> none  [the longest x1 9.4 us: inverse_table(): factor * jnp.cos(phases)]
  transfers between devices with their start and end apart: 2 -> 3, of which waited for: 2 -> 1; matrix products, arithmetic and copies ran while one was open for 2% -> 1% of each run, Pallas kernels for 0% -> 0%
where the time goes in v1:
time: 75.9 us; the launch traced here: 74.7 us
  blocking collectives  29.3 us (39%)
  starting transfers between devices  20.4 us (27%)
  Pallas kernels  9.85 us (13%)
  waiting for transfers between devices  7.61 us (10%)
  local copies, waits for them, and re-layouts  6.64 us (9%)
  other arithmetic  0.85 us (1%)
    all_to_all x1, blocking collectives, local(): all_channels = lax.all_to_all(slices, ('x', 'z', 'core'), 0, 0)  18.8 us
    all_to_all x1, starting transfers between devices, local(): own = lax.all_to_all(picked, ('x', 'z', 'y', 'zh'), 0, 0)  10.7 us
    all_gather x1, blocking collectives, local(): lax.all_gather(jnp.concatenate([rows, opposite], axis=0), 'y', axis=0)  10.5 us
    all_to_all x1, waiting for transfers between devices, local(): own = lax.all_to_all(picked, ('x', 'z', 'y', 'zh'), 0, 0)  7.61 us
    unnamed x8, local copies, waits for them, and re-layouts  6.64 us
    pallas_call x1, Pallas kernels, local(): pl.pallas_call(correlate_kernel, out_shape=jax.ShapeDtypeStruct((OWN, OWN...  6.35 us
    ppermute x1, starting transfers between devices, local(): other = lax.ppermute(own, 'core', [(0, 1), (1, 0)])  5.16 us
    ppermute x1, starting transfers between devices, local(): opposite = lax.ppermute(rows, 'zh', [(0, 1), (1, 0)])  4.57 us
  transfers between devices with their start and end apart: 3, of which 1 were waited for; matrix products, arithmetic and copies ran while one was open for 1% of the time, Pallas kernels for 0%

profile of v1, /device:TPU:1, one launch (start us, length us, event | category | flops | bytes accessed | tf_op | source)
XLA Modules:
  0.0 74.7 jit_solution(6101247748586748169)
XLA Ops:
  0.0 1.6 %shard_map.73 = (bf16[32,16,128]{2,1,0:T(8,128)(2,1)}, bf16[16,2048]{1,0:T(8,128)(2,1)}) custom-call(bf16[16,2048]{1,0:T(8,128)(2,1)} %bitcast.9, s32[1,16]{1,0:T(1,128)} %bitcast.10), custom_call_target="tpu_custom_call" | custom-call | tf_op jit(solution)/shard_map/pallas_call | solution.py:172
  1.6 18.8 %all_to_all.10.all_ref = bf16[32,16,128]{2,1,0:T(8,128)(2,1)} all-to-all(bf16[32,16,128]{2,1,0:T(8,128)(2,1)} %get-tuple-element.7), channel_id=1, replica_groups=mesh['x'=4,'z'=4,'core'=2,'y'=4,'zh'=2] {'x','z','core'}, dimensions={0} | all-to-all | bytes 262144 | tf_op jit(solution)/shard_map/all_to_all | solution.py:179
  20.5 1.9 %shard_map.74 = bf16[128,8,128]{2,1,0:T(8,128)(2,1)} custom-call(s32[1,128]{1,0:T(1,128)} %bitcast.11, bf16[32,16,128]{2,1,0:T(8,128)(2,1)} %all_to_all.10.all_ref), custom_call_target="tpu_custom_call" | custom-call | tf_op jit(solution)/shard_map/pallas_call | solution.py:182
  22.3 10.7 %all-to-all-start.1 = ((bf16[128,8,128]{2,1,0:T(8,128)(2,1)}), bf16[128,8,128]{2,1,0:T(8,128)(2,1)S(1)}, u32[]{:S(2)}, u32[]{:S(2)}) async-start(bf16[128,8,128]{2,1,0:T(8,128)(2,1)} %shard_map.74), calls=%async_computation.1 | async-start | bytes 524288 | tf_op jit(solution)/shard_map/all_to_all | solution.py:186
  33.0 4.6 %collective-permute-start.1 = (bf16[16,2048]{1,0:T(8,128)(2,1)}, bf16[16,2048]{1,0:T(8,128)(2,1)S(1)}, u32[]{:S(2)}, u32[]{:S(2)}) collective-permute-start(bf16[16,2048]{1,0:T(8,128)(2,1)} %get-tuple-element.8), channel_id=1, source_target_pairs={{0,1},{1,0},{2,3},{3,2},{4,5},{5,4},{6,7},{7,6},{8,9},{9,8},{10,11... | collective-permute-start | bytes 196616 | tf_op jit(solution)/shard_map/ppermute | solution.py:180
  37.6 7.6 %all-to-all-done.1 = bf16[128,8,128]{2,1,0:T(8,128)(2,1)S(1)} async-done(((bf16[128,8,128]{2,1,0:T(8,128)(2,1)}), bf16[128,8,128]{2,1,0:T(8,128)(2,1)S(1)}, u32[]{:S(2)}, u32[]{:S(2)}) %all-to-all-start.1) | async-done | bytes 262176 | tf_op jit(solution)/shard_map/all_to_all | solution.py:186
  45.2 5.2 %collective-permute-start = (bf16[128,8,128]{2,1,0:T(8,128)(2,1)S(1)}, bf16[128,8,128]{2,1,0:T(8,128)(2,1)S(1)}, u32[]{:S(2)}, u32[]{:S(2)}) collective-permute-start(bf16[128,8,128]{2,1,0:T(8,128)(2,1)S(1)} %all-to-all-done.1), channel_id=1, source_target_pairs={{0,8},{8,0},{1,9},{9,1},{2,10},{10,2},{3,11},{11,3},{4,12},{12,4},... | collective-permute-start | bytes 786440 | tf_op jit(solution)/shard_map/ppermute | solution.py:187
  50.4 0.0 collective-permute-done.1
  50.4 0.8 %pad_maximum_fusion = bf16[32,2048]{1,0:T(8,128)(2,1)S(1)} fusion(bf16[16,2048]{1,0:T(8,128)(2,1)S(1)} %collective-permute-done.1, bf16[16,2048]{1,0:T(8,128)(2,1)} %get-tuple-element.8), kind=kLoop, calls=%fused_computation | loop fusion | flops 262144 | bytes 262144 | tf_op jit(solution)/shard_map/concatenate | solution.py:181
  51.2 10.5 %all-gather = bf16[128,2048]{1,0:T(8,128)(2,1)S(1)} all-gather(bf16[32,2048]{1,0:T(8,128)(2,1)S(1)} %pad_maximum_fusion), channel_id=2, replica_groups=mesh['x'=4,'z'=4,'core'=2,'y'=4,'zh'=2] {'y'}, dimensions={0}, use_global_device_ids=true | all-gather | bytes 655360 | tf_op jit(solution)/shard_map/all_gather | solution.py:181
  61.7 0.0 collective-permute-done
  61.7 0.0 copy-start
  61.7 3.4 %copy-done = bf16[8,2048,256]{2,1,0:T(8,128)(2,1)S(1)} copy-done((bf16[8,2048,256]{2,1,0:T(8,128)(2,1)S(1)}, bf16[8,2048,256]{2,1,0:T(8,128)(2,1)}, u32[]{:S(2)}) %copy-start) | copy-done | bytes 8388632
  65.1 0.0 copy-start.1
  65.1 1.6 %copy-done.1 = bf16[2048,512]{1,0:T(8,128)(2,1)S(1)} copy-done((bf16[2048,512]{1,0:T(8,128)(2,1)S(1)}, bf16[2048,512]{1,0:T(8,128)(2,1)}, u32[]{:S(2)}) %copy-start.1) | copy-done | bytes 2097176
  66.7 0.0 copy-start.2
  66.7 0.9 %copy-done.2 = bf16[384,128]{1,0:T(8,128)(2,1)S(1)} copy-done((bf16[384,128]{1,0:T(8,128)(2,1)S(1)}, bf16[384,128]{1,0:T(8,128)(2,1)}, u32[]{:S(2)}) %copy-start.2) | copy-done | bytes 98328
  67.6 0.0 copy-start.3
  67.6 0.8 %copy-done.3 = f32[8,8,128]{2,1,0:T(8,128)S(1)} copy-done((f32[8,8,128]{2,1,0:T(8,128)S(1)}, f32[8,8,128]{2,1,0:T(8,128)}, u32[]{:S(2)}) %copy-start.3) | copy-done | bytes 32792
  68.4 6.4 %shard_map.75 = bf16[16,16,512]{2,1,0:T(8,128)(2,1)} custom-call(bf16[16,8,8,128]{3,2,1,0:T(8,128)(2,1)S(1)} %bitcast.7, bf16[16,8,8,128]{3,2,1,0:T(8,128)(2,1)S(1)} %bitcast.8, bf16[8,16,2048]{2,1,0:T(8,128)(2,1)S(1)} %bitcast.6, bf16[8,2048,256]{2,1,0:T(8,128)(2,1)S(1)} %copy-done, bf16[384,128]{1,0:T(8,128)(2,1)S(1)} %copy-done.2, ...), custom_call_target="tpu_custom_call" | custom-call | tf_op jit(solution)/shard_map/pallas_call | solution.py:190
Async XLA Ops:
  22.3 22.9 %all-to-all-start.1 = ((bf16[128,8,128]{2,1,0:T(8,128)(2,1)}), bf16[128,8,128]{2,1,0:T(8,128)(2,1)S(1)}, u32[]{:S(2)}, u32[]{:S(2)}) async-start(bf16[128,8,128]{2,1,0:T(8,128)(2,1)} %shard_map.74), calls=%async_computation.1 | async-start | bytes 524288 | tf_op jit(solution)/shard_map/all_to_all | solution.py:186
  33.0 17.3 %collective-permute-start.1 = (bf16[16,2048]{1,0:T(8,128)(2,1)}, bf16[16,2048]{1,0:T(8,128)(2,1)S(1)}, u32[]{:S(2)}, u32[]{:S(2)}) collective-permute-start(bf16[16,2048]{1,0:T(8,128)(2,1)} %get-tuple-element.8), channel_id=1, source_target_pairs={{0,1},{1,0},{2,3},{3,2},{4,5},{5,4},{6,7},{7,6},{8,9},{9,8},{10,11... | collective-permute-start | bytes 196616 | tf_op jit(solution)/shard_map/ppermute | solution.py:180
  45.2 16.5 %collective-permute-start = (bf16[128,8,128]{2,1,0:T(8,128)(2,1)S(1)}, bf16[128,8,128]{2,1,0:T(8,128)(2,1)S(1)}, u32[]{:S(2)}, u32[]{:S(2)}) collective-permute-start(bf16[128,8,128]{2,1,0:T(8,128)(2,1)S(1)} %all-to-all-done.1), channel_id=1, source_target_pairs={{0,8},{8,0},{1,9},{9,1},{2,10},{10,2},{3,11},{11,3},{4,12},{12,4},... | collective-permute-start | bytes 786440 | tf_op jit(solution)/shard_map/ppermute | solution.py:187
  61.7 3.4 %copy-start = (bf16[8,2048,256]{2,1,0:T(8,128)(2,1)S(1)}, bf16[8,2048,256]{2,1,0:T(8,128)(2,1)}, u32[]{:S(2)}) copy-start(bf16[8,2048,256]{2,1,0:T(8,128)(2,1)} %constant.8.clone.table_ref) | copy-start | bytes 25165828
  65.1 1.6 %copy-start.1 = (bf16[2048,512]{1,0:T(8,128)(2,1)S(1)}, bf16[2048,512]{1,0:T(8,128)(2,1)}, u32[]{:S(2)}) copy-start(bf16[2048,512]{1,0:T(8,128)(2,1)} %constant.11.clone.inverse_ref) | copy-start | bytes 6291460
  66.7 0.9 %copy-start.2 = (bf16[384,128]{1,0:T(8,128)(2,1)S(1)}, bf16[384,128]{1,0:T(8,128)(2,1)}, u32[]{:S(2)}) copy-start(bf16[384,128]{1,0:T(8,128)(2,1)} %constant.9.clone.band_ref) | copy-start | bytes 294916
  67.6 0.8 %copy-start.3 = (f32[8,8,128]{2,1,0:T(8,128)S(1)}, f32[8,8,128]{2,1,0:T(8,128)}, u32[]{:S(2)}) copy-start(f32[8,8,128]{2,1,0:T(8,128)} %constant.10.clone.share_ref) | copy-start | bytes 98308

commit v2 on v1

v2 whole, which is shorter than its diff:
```python
import functools
import math

import jax
import jax.numpy as jnp
import numpy as np
from jax import lax
from jax.experimental import pallas as pl
from jax.experimental.pallas import tpu as pltpu
from jax.sharding import Mesh
from jax.sharding import PartitionSpec as P

LENGTH = 2048
BINS = LENGTH // 2
FOLD = LENGTH // 2
HALF = 256
LAGS = 2 * HALF
SMOOTH = 32
LANES = 128
SLICES = LENGTH // LANES
BLOCKS = BINS // LANES
WINS = 8
OWN = 16
SOURCES = 128
CHANNELS = 512
HELD = WINS * 8
MARK = 1e30
MARK_LIMIT = 1e29
BF16 = jnp.bfloat16
VMEM_SPEC = pl.BlockSpec(memory_space=pltpu.VMEM)
HBM_SPEC = pl.BlockSpec(memory_space=pltpu.HBM)
F32 = jnp.float32


def bin_order():
    return np.concatenate([np.arange(0, BINS, 2), np.arange(1, BINS, 2)])


def forward_table():
    samples = np.arange(FOLD)[:, None]
    phases = (samples * bin_order()[None, :] % LENGTH).astype(np.float32) * np.float32(2.0 * math.pi / LENGTH)
    table = np.stack([np.cos(phases), -np.sin(phases)], axis=1).reshape(FOLD, 2, BLOCKS, LANES)
    return table.transpose(2, 0, 1, 3).reshape(BLOCKS, FOLD, 2 * LANES).astype(jnp.bfloat16)


def inverse_table():
    bins = bin_order()[:, None]
    lags = np.arange(LAGS)[None, :] - HALF
    phases = (bins * lags % LENGTH).astype(np.float32) * np.float32(2.0 * math.pi / LENGTH)
    factor = np.where(bins == 0, 1.0, 2.0).astype(np.float32) / np.float32(math.sqrt(LENGTH))
    table = np.stack([factor * np.cos(phases), -factor * np.sin(phases)], axis=0)
    table = table.reshape(2, BLOCKS, LANES, LAGS).transpose(1, 0, 2, 3)
    return table.reshape(BLOCKS, 2 * LANES, LAGS).astype(jnp.bfloat16)


def centre_kernel(records_ref, usable_ref, slices_ref, rows_ref):
    widened = records_ref[...].astype(F32)
    mean = jnp.sum(widened, axis=1, keepdims=True) * (1.0 / LENGTH)
    centred = widened - mean
    row_ids = lax.broadcasted_iota(jnp.int32, (OWN, OWN), 0)
    col_ids = lax.broadcasted_iota(jnp.int32, (OWN, OWN), 1)
    flags = jnp.broadcast_to(usable_ref[...].astype(F32), (OWN, OWN))
    flag = jnp.sum(jnp.where(row_ids == col_ids, flags, 0.0), axis=1, keepdims=True)
    marked = jnp.where(flag > 0.5, centred, MARK).astype(BF16)
    rows_ref[...] = marked
    for part in range(SLICES):
        piece = marked[:, part * LANES : (part + 1) * LANES]
        slices_ref[2 * part] = piece
        slices_ref[2 * part + 1] = piece


def pick_kernel(sources_ref, all_ref, rows_ref, opposite_ref, picked_ref, pair_ref, token_ref):
    pair_ref[:OWN] = rows_ref[...]
    pair_ref[OWN:] = opposite_ref[...]
    core = lax.axis_index("core")
    rows = all_ref[...].reshape(CHANNELS, LANES)
    channel_ids = lax.broadcasted_iota(jnp.int32, (CHANNELS, SOURCES), 0)
    onehot = (channel_ids == sources_ref[...]).astype(F32).astype(BF16)
    picked = lax.dot_general(
        onehot, rows, (((0,), (0,)), ((), ())), preferred_element_type=F32
    ).reshape(WINS, 2, 8, LANES)
    half = jnp.where(core == 0, picked[:, 0], picked[:, 1]).astype(BF16)
    for place in range(SLICES):
        picked_ref[pl.ds(place * WINS, WINS)] = half
    token_ref[...] = jnp.zeros((8, LANES), F32)


def load_kernel(token_ref, table_hbm, table_ref, sem):
    del token_ref
    copy = pltpu.make_async_copy(table_hbm, table_ref, sem)
    copy.start()
    copy.wait()


def unmark(values):
    widened = values.astype(F32)
    return jnp.where(widened > MARK_LIMIT, 0.0, widened)


def usable_lanes(values):
    return (values.astype(F32) < MARK_LIMIT).astype(F32)


def store_folded(even, odd, where, lanes, low, high):
    low, high = unmark(low), unmark(high)
    even[where, lanes] = (low + high).astype(BF16)
    odd[where, lanes] = (low - high).astype(BF16)


def store_sources(ref, even, odd):
    for part in range(SLICES // 2):
        low = ref[part].reshape(HELD, LANES)
        high = ref[part + SLICES // 2].reshape(HELD, LANES)
        store_folded(even, odd, pl.ds(0, HELD), pl.ds(part * LANES, LANES), low, high)


def band_matrices():
    rows = lax.broadcasted_iota(jnp.int32, (2 * LANES, 2 * LANES), 0)
    cols = lax.broadcasted_iota(jnp.int32, (2 * LANES, 2 * LANES), 1)
    apart = 2 * (rows - cols)
    return {
        (shift, step): (jnp.abs(apart + shift + 4 * LANES * step) <= SMOOTH).astype(F32).astype(BF16)
        for shift in (-1, 0, 1)
        for step in (-1, 0, 1)
    }


def whiten(even, odd, even_table, odd_table, spec, amp, before_odd):
    bands = band_matrices()
    for block in range(BLOCKS):
        if block == BLOCKS // 2:
            before_odd()
        folded, table = (even, even_table) if block < BLOCKS // 2 else (odd, odd_table)
        part = jnp.dot(folded[...], table[block % (BLOCKS // 2)], preferred_element_type=F32)
        spec[block] = part
        real, imag = part[:, :LANES], part[:, LANES:]
        amp[:, pl.ds(block * LANES, LANES)] = jnp.sqrt(real * real + imag * imag).astype(BF16)

    lane_ids = lax.broadcasted_iota(jnp.int32, (1, 2 * LANES), 1)
    for pair in range(BLOCKS // 2):
        parity, place = divmod(pair, 2)
        total = None
        for other in range(4):
            near = jnp.dot(
                amp[:, pl.ds(other * 2 * LANES, 2 * LANES)],
                bands[other // 2 - parity, other % 2 - place],
                preferred_element_type=F32,
            )
            total = near if total is None else total + near
        bin_ids = 2 * (lane_ids + place * 2 * LANES) + parity
        count = jnp.minimum(bin_ids, SMOOTH) + jnp.minimum(BINS - 1 - bin_ids, SMOOTH) + 1
        scale = 1.0 / (total * (1.0 / count.astype(F32)) + 1e-6)
        for half in range(2):
            block = 2 * pair + half
            piece = scale[:, half * LANES : (half + 1) * LANES]
            spec[block, :, :LANES] = spec[block, :, :LANES] * piece
            spec[block, :, LANES:] = spec[block, :, LANES:] * piece


def whiten_kernel(
    own_ref, pair_ref, next1_ref, next2_ref, next3_ref, even_table, odd_hbm,
    spec, send, flags, odd_table, even, odd, amp, sem,
):
    odd_copy = pltpu.make_async_copy(odd_hbm, odd_table, sem)
    odd_copy.start()
    line = lax.axis_index("y")
    side = lax.axis_index("zh")
    store_sources(own_ref, even, odd)
    for step, ref in enumerate((pair_ref, next1_ref, next2_ref, next3_ref)):
        for swap in range(2):
            win = lax.rem(line + 4 - step, 4) * 2 + lax.rem(side + swap, 2)
            first = pl.multiple_of(win * OWN, OWN)
            received = ref[swap * OWN : swap * OWN + OWN, :]
            where = pl.ds(HELD + first, OWN)
            store_folded(even, odd, where, slice(None), received[:, :FOLD], received[:, FOLD:])
            flags[pl.ds(first, OWN), :] = usable_lanes(received[:, :LANES])
    whiten(even, odd, even_table, odd_table, spec, amp, odd_copy.wait)
    send[:BLOCKS] = spec[:, :HELD, :].astype(BF16)
    usable = usable_lanes(own_ref[0].reshape(HELD, LANES)).astype(BF16)
    send[BLOCKS, :, :LANES] = usable
    send[BLOCKS, :, LANES:] = usable


def correlate(sources, flags, ready, rec_flags, inverse, store, held, added, cross, before_inverse):
    held[...] = sources[:BLOCKS].astype(F32)
    added[...] = held[:, :, :LANES] + held[:, :, LANES:]

    def one_block(block, carry):
        for part in range(0, OWN, 8):
            rows = [pl.ds(HELD + w * OWN + part, 8) for w in range(WINS)]
            rec_re = [ready[block, where, :LANES] for where in rows]
            rec_im = [ready[block, where, LANES:] for where in rows]
            rec_sum = [re + im for re, im in zip(rec_re, rec_im)]
            rec_gap = [re - im for re, im in zip(rec_re, rec_im)]
            for index in range(8):
                sums = [None, None, None]
                for w in range(WINS):
                    row = w * 8 + index
                    src_re = jnp.broadcast_to(held[block, row : row + 1, :LANES], (8, LANES))
                    src_im = jnp.broadcast_to(held[block, row : row + 1, LANES:], (8, LANES))
                    src_sum = jnp.broadcast_to(added[block, row : row + 1, :], (8, LANES))
                    terms = (src_sum * rec_re[w], src_im * rec_gap[w], src_re * rec_sum[w])
                    sums = [term if acc is None else acc + term for acc, term in zip(sums, terms)]
                where = pl.ds(index * OWN + part, 8)
                cross[block, where, :LANES] = (sums[0] - sums[1]).astype(BF16)
                cross[block, where, LANES:] = (sums[0] - sums[2]).astype(BF16)
        return carry

    lax.fori_loop(0, BLOCKS, one_block, 0)
    before_inverse()
    lagged = jnp.dot(cross[0], inverse[0], preferred_element_type=F32)
    for block in range(1, BLOCKS):
        lagged += jnp.dot(cross[block], inverse[block], preferred_element_type=F32)
    for index in range(8):
        count = jnp.zeros((OWN, LANES), F32)
        for w in range(WINS):
            row = w * 8 + index
            source = jnp.broadcast_to(flags[row : row + 1, :], (OWN, LANES))
            count += source * rec_flags[w * OWN : w * OWN + OWN, :]
        scale = lax.rsqrt(jnp.maximum(count, 1.0))
        for piece in range(LAGS // LANES):
            lanes = slice(piece * LANES, (piece + 1) * LANES)
            store(index, lanes, (lagged[index * OWN : index * OWN + OWN, lanes] * scale).astype(BF16))


def own_kernel(send, ready, rec_flags, inverse_hbm, own_lags, inverse, held, added, cross, sem):
    inverse_copy = pltpu.make_async_copy(inverse_hbm, inverse, sem)
    inverse_copy.start()

    def store(index, lanes, values):
        own_lags[index, :, lanes] = values

    usable = send[BLOCKS, :, :LANES].astype(F32)
    correlate(send, usable, ready, rec_flags, inverse, store, held, added, cross, inverse_copy.wait)


def other_kernel(received, ready, rec_flags, inverse, own_lags, out_ref, held, added, cross):
    core = lax.axis_index("core")
    out_ref[pl.ds(core * 8, 8)] = own_lags[...]

    def store(index, lanes, values):
        out_ref[(1 - core) * 8 + index, :, lanes] = values

    usable = received[BLOCKS, :, :LANES].astype(F32)
    correlate(received, usable, ready, rec_flags, inverse, store, held, added, cross, lambda: None)


def in_vmem(value):
    return pltpu.with_memory_space_constraint(value, pltpu.VMEM)


def in_hbm(value):
    return pltpu.with_memory_space_constraint(jnp.asarray(value), pltpu.HBM)


def local(records, usable, sources):
    rows_in = records.reshape(OWN, LENGTH)
    slices, rows = pl.pallas_call(
        centre_kernel,
        out_specs=[VMEM_SPEC] * 2,
        out_shape=(pltpu.VMEM((2 * SLICES, OWN, LANES), BF16), pltpu.VMEM((OWN, LENGTH), BF16)),
    )(rows_in, usable.reshape(1, OWN))
    all_channels = lax.all_to_all(slices, ("x", "z", "core"), 0, 0)
    opposite = lax.ppermute(rows, "zh", [(0, 1), (1, 0)])
    picked, pair, token = pl.pallas_call(
        pick_kernel,
        in_specs=[VMEM_SPEC] * 4,
        out_specs=[VMEM_SPEC] * 3,
        out_shape=(
            pltpu.VMEM((SLICES * WINS, 8, LANES), BF16),
            pltpu.VMEM((2 * OWN, LENGTH), BF16),
            pltpu.VMEM((8, LANES), F32),
        ),
    )(sources.reshape(1, SOURCES), in_vmem(all_channels), in_vmem(rows), in_vmem(opposite))
    table = pl.pallas_call(
        load_kernel,
        in_specs=[VMEM_SPEC, HBM_SPEC],
        out_specs=VMEM_SPEC,
        out_shape=pltpu.VMEM((BLOCKS // 2, FOLD, 2 * LANES), BF16),
        scratch_shapes=[pltpu.SemaphoreType.DMA(())],
        compiler_params=pltpu.CompilerParams(vmem_limit_bytes=2**20),
    )(token, in_hbm(forward_table()[: BLOCKS // 2]))
    nexts = [lax.ppermute(pair, "y", [(i, (i + k) % 4) for i in range(4)]) for k in (1, 2, 3)]
    own = lax.all_to_all(picked, ("x", "z", "y", "zh"), 0, 0)
    own, nexts, table = lax.optimization_barrier((own, nexts, table))
    own = own.reshape(SLICES, WINS, 8, LANES)
    rows = HELD + WINS * OWN
    limit = pltpu.CompilerParams(vmem_limit_bytes=16 * 2**20)
    ready, send, flags = pl.pallas_call(
        whiten_kernel,
        in_specs=[VMEM_SPEC] * 6 + [HBM_SPEC],
        out_specs=[VMEM_SPEC] * 3,
        out_shape=(
            pltpu.VMEM((BLOCKS, rows, 2 * LANES), F32),
            pltpu.VMEM((BLOCKS + 1, HELD, 2 * LANES), BF16),
            pltpu.VMEM((WINS * OWN, LANES), F32),
        ),
        scratch_shapes=[
            pltpu.VMEM((BLOCKS // 2, FOLD, 2 * LANES), BF16),
            pltpu.VMEM((rows, FOLD), BF16),
            pltpu.VMEM((rows, FOLD), BF16),
            pltpu.VMEM((rows, BINS), BF16),
            pltpu.SemaphoreType.DMA(()),
        ],
        compiler_params=limit,
    )(
        *(in_vmem(value) for value in (own, pair, *nexts, table)),
        in_hbm(forward_table()[BLOCKS // 2 :]),
    )
    received = lax.ppermute(send, "core", [(0, 1), (1, 0)])
    scratch = [
        pltpu.VMEM((BLOCKS, HELD, 2 * LANES), F32),
        pltpu.VMEM((BLOCKS, HELD, LANES), F32),
        pltpu.VMEM((BLOCKS, 8 * OWN, 2 * LANES), BF16),
    ]
    own_lags, inverse = pl.pallas_call(
        own_kernel,
        in_specs=[VMEM_SPEC] * 3 + [HBM_SPEC],
        out_specs=[VMEM_SPEC] * 2,
        out_shape=(pltpu.VMEM((8, OWN, LAGS), BF16), pltpu.VMEM((BLOCKS, 2 * LANES, LAGS), BF16)),
        scratch_shapes=[*scratch, pltpu.SemaphoreType.DMA(())],
        compiler_params=limit,
    )(*(in_vmem(value) for value in (send, ready, flags)), in_hbm(inverse_table()))
    return pl.pallas_call(
        other_kernel,
        out_shape=jax.ShapeDtypeStruct((OWN, OWN, LAGS), BF16),
        in_specs=[VMEM_SPEC] * 5,
        scratch_shapes=scratch,
        compiler_params=limit,
    )(*(in_vmem(value) for value in (received, ready, flags, inverse, own_lags)))


def solution(mesh):
    split = Mesh(mesh.devices.reshape(4, 4, 2, 4, 2), ("x", "z", "core", "y", "zh"))
    recv, win = ("x", "z", "core"), ("y", "zh")
    in_specs = (P(recv, win, None), P(recv, win), P())
    out_specs = P(win, recv, None)
    return jax.shard_map(local, mesh=split, in_specs=in_specs, out_specs=out_specs, check_vma=False)
```

time: 75.9 us -> 58.9 us (0.78); the launches traced: 74.7 us -> 58.6 us
  blocking collectives: 29.3 us -> 0 us
  starting transfers between devices: 20.4 us -> 32.5 us
  local copies, waits for them, and re-layouts: 6.64 us -> 0 us
  waiting for transfers between devices: 7.61 us -> 13.7 us
  Pallas kernels: 9.85 us -> 12.3 us
  other arithmetic: 0.85 us -> 0 us
    all_to_all x1 -> x0, blocking collectives: 18.8 us -> none  [local(): all_channels = lax.all_to_all(slices, ('x', 'z', 'core'), 0, 0)]
    all_gather x1 -> x0, blocking collectives: 10.5 us -> none  [local(): lax.all_gather(jnp.concatenate([rows, opposite], axis=0), 'y', axis=0)]
    all_to_all x0 -> x1, starting transfers between devices: none -> 10 us  [local(): all_channels = lax.all_to_all(slices, ('x', 'z', 'core'), 0, 0)]
    ppermute x1 -> x4, waiting for transfers between devices: 0.01 us -> 9.22 us  [the longest x3 9.22 us: local(): lax.ppermute(pair, 'y', [(i, (i + k) % 4) for i in range(4)])]
    all_to_all x1, waiting for transfers between devices: 7.61 us -> 0.01 us  [local(): own = lax.all_to_all(picked, ('x', 'z', 'y', 'zh'), 0, 0)]
    unnamed x8 -> x0, local copies, waits for them, and re-layouts: 6.64 us -> none
    ppermute x1, waiting for transfers between devices: 0.01 us -> 4.47 us  [local(): opposite = lax.ppermute(rows, 'zh', [(0, 1), (1, 0)])]
    all_to_all x1, starting transfers between devices: 10.7 us -> 13.5 us  [local(): own = lax.all_to_all(picked, ('x', 'z', 'y', 'zh'), 0, 0)]
  transfers between devices with their start and end apart: 3 -> 7, of which waited for: 1 -> 5; matrix products, arithmetic and copies ran while one was open for 1% -> 0% of each run, Pallas kernels for 0% -> 6%
where the time goes in v2:
time: 58.9 us; the launch traced here: 58.6 us
  starting transfers between devices  32.5 us (55%)
  waiting for transfers between devices  13.7 us (23%)
  Pallas kernels  12.3 us (21%)
    all_to_all x1, starting transfers between devices, local(): own = lax.all_to_all(picked, ('x', 'z', 'y', 'zh'), 0, 0)  13.5 us
    all_to_all x1, starting transfers between devices, local(): all_channels = lax.all_to_all(slices, ('x', 'z', 'core'), 0, 0)  10 us
    ppermute x3, waiting for transfers between devices, local(): lax.ppermute(pair, 'y', [(i, (i + k) % 4) for i in range(4)])  9.22 us
    ppermute x1, waiting for transfers between devices, local(): opposite = lax.ppermute(rows, 'zh', [(0, 1), (1, 0)])  4.47 us
    ppermute x1, starting transfers between devices, local(): opposite = lax.ppermute(rows, 'zh', [(0, 1), (1, 0)])  4.3 us
    pallas_call x1, Pallas kernels, local(): pl.pallas_call(whiten_kernel, in_specs=[VMEM_SPEC] * 6 + [HBM_SPEC], out_...  3.31 us
    ppermute x3, starting transfers between devices, local(): lax.ppermute(pair, 'y', [(i, (i + k) % 4) for i in range(4)])  3.02 us
    pallas_call x1, Pallas kernels, local(): pl.pallas_call(other_kernel, out_shape=jax.ShapeDtypeStruct((OWN, OWN, LA...  2.13 us
  transfers between devices with their start and end apart: 7, of which 5 were waited for; matrix products, arithmetic and copies ran while one was open for 0% of the time, Pallas kernels for 6%

profile of v2, /device:TPU:1, one launch (start us, length us, event | category | flops | bytes accessed | tf_op | source)
XLA Modules:
  0.0 58.6 jit_solution(1124245707603916712)
XLA Ops:
  0.0 1.6 %shard_map.64 = (bf16[32,16,128]{2,1,0:T(8,128)(2,1)}, bf16[16,2048]{1,0:T(8,128)(2,1)S(1)}) custom-call(bf16[16,2048]{1,0:T(8,128)(2,1)} %bitcast.5, s32[1,16]{1,0:T(1,128)} %bitcast.6), custom_call_target="tpu_custom_call" | custom-call | tf_op jit(solution)/shard_map/pallas_call | solution.py:258
  1.6 10.0 %all-to-all-start = ((bf16[32,16,128]{2,1,0:T(8,128)(2,1)}), bf16[32,16,128]{2,1,0:T(8,128)(2,1)S(1)}, u32[]{:S(2)}, u32[]{:S(2)}) async-start(bf16[32,16,128]{2,1,0:T(8,128)(2,1)} %get-tuple-element.20), calls=%async_computation | async-start | bytes 262144 | tf_op jit(solution)/shard_map/all_to_all | solution.py:263
  11.6 4.3 %collective-permute-start = (bf16[16,2048]{1,0:T(8,128)(2,1)S(1)}, bf16[16,2048]{1,0:T(8,128)(2,1)S(1)}, u32[]{:S(2)}, u32[]{:S(2)}) collective-permute-start(bf16[16,2048]{1,0:T(8,128)(2,1)S(1)} %get-tuple-element.21.rows_ref), channel_id=1, source_target_pairs={{0,1},{1,0},{2,3},{3,2},{4,5},{5,4},{6,7},{7,6},{8,9},{9,8},{10,11... | collective-permute-start | bytes 196616 | tf_op jit(solution)/shard_map/ppermute | solution.py:264
  15.9 4.5 %collective-permute-done.opposite_ref = bf16[16,2048]{1,0:T(8,128)(2,1)S(1)} collective-permute-done((bf16[16,2048]{1,0:T(8,128)(2,1)S(1)}, bf16[16,2048]{1,0:T(8,128)(2,1)S(1)}, u32[]{:S(2)}, u32[]{:S(2)}) %collective-permute-start) | collective-permute-done | bytes 65568 | tf_op jit(solution)/shard_map/ppermute | solution.py:264
  20.4 0.1 all-to-all-done.all_ref
  20.5 1.6 %shard_map.65 = (bf16[128,8,128]{2,1,0:T(8,128)(2,1)}, bf16[32,2048]{1,0:T(8,128)(2,1)S(1)}, f32[8,128]{1,0:T(8,128)S(1)}) custom-call(s32[1,128]{1,0:T(1,128)} %bitcast.7, bf16[32,16,128]{2,1,0:T(8,128)(2,1)S(1)} %all-to-all-done.all_ref, bf16[16,2048]{1,0:T(8,128)(2,1)S(1)} %get-tuple-element.21.rows_ref, ...), custom_call_target="tpu_custom_call" | custom-call | tf_op jit(solution)/shard_map/pallas_call | solution.py:265
  22.1 13.5 %all-to-all-start.1 = ((bf16[128,8,128]{2,1,0:T(8,128)(2,1)}), bf16[128,8,128]{2,1,0:T(8,128)(2,1)S(1)}, u32[]{:S(2)}, u32[]{:S(2)}) async-start(bf16[128,8,128]{2,1,0:T(8,128)(2,1)} %get-tuple-element.22), calls=%async_computation.1 | async-start | bytes 524288 | tf_op jit(solution)/shard_map/all_to_all | solution.py:284
  35.6 1.9 %collective-permute-start.3 = (bf16[32,2048]{1,0:T(8,128)(2,1)S(1)}, bf16[32,2048]{1,0:T(8,128)(2,1)S(1)}, u32[]{:S(2)}, u32[]{:S(2)}) collective-permute-start(bf16[32,2048]{1,0:T(8,128)(2,1)S(1)} %get-tuple-element.23.pair_ref), channel_id=1, source_target_pairs={{0,6},{2,0},{4,2},{6,4},{1,7},{3,1},{5,3},{7,5},{8,14},{10,8},{12,... | collective-permute-start | bytes 393224 | tf_op jit(solution)/shard_map/ppermute | solution.py:283
  37.5 0.6 collective-permute-start.2
  38.1 0.6 collective-permute-start.1
  38.6 1.6 %shard_map.66.even_table = bf16[4,1024,256]{2,1,0:T(8,128)(2,1)S(1)} custom-call(f32[8,128]{1,0:T(8,128)S(1)} %get-tuple-element.24.token_ref, bf16[4,1024,256]{2,1,0:T(8,128)(2,1)} %constant.6.clone.table_hbm), custom_call_target="tpu_custom_call" | custom-call | tf_op jit(solution)/shard_map/pallas_call | solution.py:275
  40.2 0.3 collective-permute-done.3.next3_ref
  40.6 3.6 %collective-permute-done.2.next2_ref = bf16[32,2048]{1,0:T(8,128)(2,1)S(1)} collective-permute-done((bf16[32,2048]{1,0:T(8,128)(2,1)S(1)}, bf16[32,2048]{1,0:T(8,128)(2,1)S(1)}, u32[]{:S(2)}, u32[]{:S(2)}) %collective-permute-start.2) | collective-permute-done | bytes 131104 | tf_op jit(solution)/shard_map/ppermute | solution.py:283
  44.2 5.3 %collective-permute-done.1.next1_ref = bf16[32,2048]{1,0:T(8,128)(2,1)S(1)} collective-permute-done((bf16[32,2048]{1,0:T(8,128)(2,1)S(1)}, bf16[32,2048]{1,0:T(8,128)(2,1)S(1)}, u32[]{:S(2)}, u32[]{:S(2)}) %collective-permute-start.1) | collective-permute-done | bytes 131104 | tf_op jit(solution)/shard_map/ppermute | solution.py:283
  49.5 0.0 all-to-all-done.1
  49.5 3.3 %shard_map.67 = (f32[8,192,256]{2,1,0:T(8,128)S(1)}, bf16[9,64,256]{2,1,0:T(8,128)(2,1)S(1)}, f32[128,128]{1,0:T(8,128)S(1)}) custom-call(bf16[16,8,8,128]{3,2,1,0:T(8,128)(2,1)S(1)} %bitcast.4, bf16[32,2048]{1,0:T(8,128)(2,1)S(1)} %get-tuple-element.23.pair_ref, bf16[32,2048]{1,0:T(8,128)(2,1)S(1)} %collective-permute-done.1.next1_ref, ...), custom_call_target="tpu_custom_call" | custom-call | tf_op jit(solution)/shard_map/pallas_call | solution.py:289
  52.8 1.6 %collective-permute-start.4 = (bf16[9,64,256]{2,1,0:T(8,128)(2,1)S(1)}, bf16[9,64,256]{2,1,0:T(8,128)(2,1)S(1)}, u32[]{:S(2)}, u32[]{:S(2)}) collective-permute-start(bf16[9,64,256]{2,1,0:T(8,128)(2,1)S(1)} %get-tuple-element.30.send), channel_id=1, source_target_pairs={{0,8},{8,0},{1,9},{9,1},{2,10},{10,2},{3,11},{11,3},{4,12},{12,4},... | collective-permute-start | bytes 884744 | tf_op jit(solution)/shard_map/ppermute | solution.py:310
  54.4 2.0 %shard_map.68 = (bf16[8,16,512]{2,1,0:T(8,128)(2,1)S(1)}, bf16[8,256,512]{2,1,0:T(8,128)(2,1)S(1)}) custom-call(bf16[9,64,256]{2,1,0:T(8,128)(2,1)S(1)} %get-tuple-element.30.send, f32[8,192,256]{2,1,0:T(8,128)S(1)} %get-tuple-element.31.ready, f32[128,128]{1,0:T(8,128)S(1)} %get-tuple-element.32.rec_flags, bf16[8,256,512]{2,1,0:T(8,128)(2,1)} %constant.8.clone.inverse_hbm), custom_call_target="tpu_custom_call" | custom-call | tf_op jit(solution)/shard_map/pallas_call | solution.py:316
  56.4 0.0 collective-permute-done.4.received
  56.4 2.1 %shard_map.69 = bf16[16,16,512]{2,1,0:T(8,128)(2,1)} custom-call(bf16[9,64,256]{2,1,0:T(8,128)(2,1)S(1)} %collective-permute-done.4.received, f32[8,192,256]{2,1,0:T(8,128)S(1)} %get-tuple-element.31.ready, f32[128,128]{1,0:T(8,128)S(1)} %get-tuple-element.32.rec_flags, bf16[8,256,512]{2,1,0:T(8,128)(2,1)S(1)} %get-tuple-element.33.inverse, ...), custom_call_target="tpu_custom_call" | custom-call | tf_op jit(solution)/shard_map/pallas_call | solution.py:324
Async XLA Ops:
  1.6 18.9 %all-to-all-start = ((bf16[32,16,128]{2,1,0:T(8,128)(2,1)}), bf16[32,16,128]{2,1,0:T(8,128)(2,1)S(1)}, u32[]{:S(2)}, u32[]{:S(2)}) async-start(bf16[32,16,128]{2,1,0:T(8,128)(2,1)} %get-tuple-element.20), calls=%async_computation | async-start | bytes 262144 | tf_op jit(solution)/shard_map/all_to_all | solution.py:263
  11.6 8.8 %collective-permute-start = (bf16[16,2048]{1,0:T(8,128)(2,1)S(1)}, bf16[16,2048]{1,0:T(8,128)(2,1)S(1)}, u32[]{:S(2)}, u32[]{:S(2)}) collective-permute-start(bf16[16,2048]{1,0:T(8,128)(2,1)S(1)} %get-tuple-element.21.rows_ref), channel_id=1, source_target_pairs={{0,1},{1,0},{2,3},{3,2},{4,5},{5,4},{6,7},{7,6},{8,9},{9,8},{10,11... | collective-permute-start | bytes 196616 | tf_op jit(solution)/shard_map/ppermute | solution.py:264
  22.1 27.4 %all-to-all-start.1 = ((bf16[128,8,128]{2,1,0:T(8,128)(2,1)}), bf16[128,8,128]{2,1,0:T(8,128)(2,1)S(1)}, u32[]{:S(2)}, u32[]{:S(2)}) async-start(bf16[128,8,128]{2,1,0:T(8,128)(2,1)} %get-tuple-element.22), calls=%async_computation.1 | async-start | bytes 524288 | tf_op jit(solution)/shard_map/all_to_all | solution.py:284
  35.6 4.9 %collective-permute-start.3 = (bf16[32,2048]{1,0:T(8,128)(2,1)S(1)}, bf16[32,2048]{1,0:T(8,128)(2,1)S(1)}, u32[]{:S(2)}, u32[]{:S(2)}) collective-permute-start(bf16[32,2048]{1,0:T(8,128)(2,1)S(1)} %get-tuple-element.23.pair_ref), channel_id=1, source_target_pairs={{0,6},{2,0},{4,2},{6,4},{1,7},{3,1},{5,3},{7,5},{8,14},{10,8},{12,... | collective-permute-start | bytes 393224 | tf_op jit(solution)/shard_map/ppermute | solution.py:283
  37.5 6.7 %collective-permute-start.2 = (bf16[32,2048]{1,0:T(8,128)(2,1)S(1)}, bf16[32,2048]{1,0:T(8,128)(2,1)S(1)}, u32[]{:S(2)}, u32[]{:S(2)}) collective-permute-start(bf16[32,2048]{1,0:T(8,128)(2,1)S(1)} %get-tuple-element.23.pair_ref), channel_id=1, source_target_pairs={{0,4},{2,6},{4,0},{6,2},{1,5},{3,7},{5,1},{7,3},{8,12},{10,14},{12... | collective-permute-start | bytes 393224 | tf_op jit(solution)/shard_map/ppermute | solution.py:283
  38.1 11.4 %collective-permute-start.1 = (bf16[32,2048]{1,0:T(8,128)(2,1)S(1)}, bf16[32,2048]{1,0:T(8,128)(2,1)S(1)}, u32[]{:S(2)}, u32[]{:S(2)}) collective-permute-start(bf16[32,2048]{1,0:T(8,128)(2,1)S(1)} %get-tuple-element.23.pair_ref), channel_id=1, source_target_pairs={{0,2},{2,4},{4,6},{6,0},{1,3},{3,5},{5,7},{7,1},{8,10},{10,12},{12... | collective-permute-start | bytes 393224 | tf_op jit(solution)/shard_map/ppermute | solution.py:283
  52.8 3.6 %collective-permute-start.4 = (bf16[9,64,256]{2,1,0:T(8,128)(2,1)S(1)}, bf16[9,64,256]{2,1,0:T(8,128)(2,1)S(1)}, u32[]{:S(2)}, u32[]{:S(2)}) collective-permute-start(bf16[9,64,256]{2,1,0:T(8,128)(2,1)S(1)} %get-tuple-element.30.send), channel_id=1, source_target_pairs={{0,8},{8,0},{1,9},{9,1},{2,10},{10,2},{3,11},{11,3},{4,12},{12,4},... | collective-permute-start | bytes 884744 | tf_op jit(solution)/shard_map/ppermute | solution.py:310

commit v3 on v2

--- a/solution.py
+++ b/solution.py
@@ -24,6 +24,7 @@
 SOURCES = 128
 CHANNELS = 512
 HELD = WINS * 8
+EARLY = 5
 MARK = 1e30
 MARK_LIMIT = 1e29
 BF16 = jnp.bfloat16
@@ -33,14 +34,26 @@
 
 
 def bin_order():
-    return np.concatenate([np.arange(0, BINS, 2), np.arange(1, BINS, 2)])
+    lower = np.arange(BINS // 2)
+    upper = BINS - lower
+    upper[0] = BINS // 2
+    return np.concatenate([lower, upper])
 
 
 def forward_table():
-    samples = np.arange(FOLD)[:, None]
-    phases = (samples * bin_order()[None, :] % LENGTH).astype(np.float32) * np.float32(2.0 * math.pi / LENGTH)
-    table = np.stack([np.cos(phases), -np.sin(phases)], axis=1).reshape(FOLD, 2, BLOCKS, LANES)
-    return table.transpose(2, 0, 1, 3).reshape(BLOCKS, FOLD, 2 * LANES).astype(jnp.bfloat16)
+    samples = np.arange(LENGTH).reshape(FOLD, 2).T[:, :, None]
+    bins = np.arange(BINS // 2)[None, None, :]
+
+    def angle(product):
+        return (product % LENGTH).astype(np.float32) * np.float32(2.0 * math.pi / LENGTH)
+
+    phases = angle(samples * bins)
+    real, imag = np.cos(phases), -np.sin(phases)
+    middle = angle(samples[:, :, 0] * (BINS // 2))
+    imag[0, :, 0] = np.cos(middle[0])
+    imag[1, :, 0] = -np.sin(middle[1])
+    table = np.stack([real, imag], axis=2).reshape(2, FOLD, 2, BLOCKS // 2, LANES)
+    return table.transpose(3, 0, 1, 2, 4).reshape(BLOCKS, FOLD, 2 * LANES).astype(jnp.bfloat16)
 
 
 def inverse_table():
@@ -62,6 +75,18 @@
     flags = jnp.broadcast_to(usable_ref[...].astype(F32), (OWN, OWN))
     flag = jnp.sum(jnp.where(row_ids == col_ids, flags, 0.0), axis=1, keepdims=True)
     marked = jnp.where(flag > 0.5, centred, MARK).astype(BF16)
+    wide = 2 * LANES
+    from_ids = lax.broadcasted_iota(jnp.int32, (wide, wide), 0)
+    to_ids = lax.broadcasted_iota(jnp.int32, (wide, wide), 1)
+    taken = jnp.where(to_ids < LANES, 2 * to_ids, 2 * (to_ids - LANES) + 1)
+    move = (from_ids == taken).astype(F32).astype(BF16)
+    marked = jnp.concatenate(
+        [
+            jnp.dot(marked[:, p : p + wide], move, preferred_element_type=F32).astype(BF16)
+            for p in range(0, LENGTH, wide)
+        ],
+        axis=1,
+    )
     rows_ref[...] = marked
     for part in range(SLICES):
         piece = marked[:, part * LANES : (part + 1) * LANES]
@@ -94,60 +119,75 @@
 
 def unmark(values):
     widened = values.astype(F32)
-    return jnp.where(widened > MARK_LIMIT, 0.0, widened)
+    return jnp.where(widened > MARK_LIMIT, 0.0, widened).astype(BF16)
 
 
 def usable_lanes(values):
     return (values.astype(F32) < MARK_LIMIT).astype(F32)
 
 
-def store_folded(even, odd, where, lanes, low, high):
-    low, high = unmark(low), unmark(high)
-    even[where, lanes] = (low + high).astype(BF16)
-    odd[where, lanes] = (low - high).astype(BF16)
-
-
-def store_sources(ref, even, odd):
-    for part in range(SLICES // 2):
-        low = ref[part].reshape(HELD, LANES)
-        high = ref[part + SLICES // 2].reshape(HELD, LANES)
-        store_folded(even, odd, pl.ds(0, HELD), pl.ds(part * LANES, LANES), low, high)
-
-
-def band_matrices():
+def band_tiles():
     rows = lax.broadcasted_iota(jnp.int32, (2 * LANES, 2 * LANES), 0)
     cols = lax.broadcasted_iota(jnp.int32, (2 * LANES, 2 * LANES), 1)
-    apart = 2 * (rows - cols)
+    low, last = 2 * LANES, 2 * LANES - SMOOTH
+
+    def tile(inside):
+        return inside.astype(F32).astype(BF16)
+
+    near = jnp.abs(rows - cols) <= SMOOTH
+    below = jnp.abs(rows - cols - low) <= SMOOTH
+    above = jnp.abs(rows - cols + low) <= SMOOTH
+    row_middle, col_middle = (rows == 0) & (cols >= last), (cols == 0) & (rows >= last)
+    alone = (rows == 0) == (cols == 0)
+    same = tile(near)
+    facing = tile(rows + cols >= 2 * low - SMOOTH)
     return {
-        (shift, step): (jnp.abs(apart + shift + 4 * LANES * step) <= SMOOTH).astype(F32).astype(BF16)
-        for shift in (-1, 0, 1)
-        for step in (-1, 0, 1)
+        (0, 0): same, (0, 1): tile(below), (1, 0): tile(above), (1, 1): same,
+        (2, 2): tile(near & alone), (2, 3): tile(below | row_middle), (3, 2): tile(above | col_middle),
+        (3, 3): same, (1, 3): facing, (3, 1): facing, (1, 2): tile(col_middle), (2, 1): tile(row_middle),
     }
 
 
-def whiten(even, odd, even_table, odd_table, spec, amp, before_odd):
-    bands = band_matrices()
-    for block in range(BLOCKS):
-        if block == BLOCKS // 2:
-            before_odd()
-        folded, table = (even, even_table) if block < BLOCKS // 2 else (odd, odd_table)
-        part = jnp.dot(folded[...], table[block % (BLOCKS // 2)], preferred_element_type=F32)
-        spec[block] = part
-        real, imag = part[:, :LANES], part[:, LANES:]
-        amp[:, pl.ds(block * LANES, LANES)] = jnp.sqrt(real * real + imag * imag).astype(BF16)
-
-    lane_ids = lax.broadcasted_iota(jnp.int32, (1, 2 * LANES), 1)
+def whiten(even, odd, early_table, late_table, late_copies, spec, amp):
+    bands = band_tiles()
+    lane_ids = lax.broadcasted_iota(jnp.int32, (1, LANES), 1)
+
+    def table(place):
+        if place < EARLY:
+            return early_table[place]
+        late_copies[place - EARLY].wait()
+        return late_table[place - EARLY]
+
+    for block in range(BLOCKS // 2):
+        evens = jnp.dot(even[...], table(2 * block), preferred_element_type=F32)
+        odds = jnp.dot(odd[...], table(2 * block + 1), preferred_element_type=F32)
+        lower, upper = evens + odds, evens - odds
+        lower_re, lower_im = lower[:, :LANES], lower[:, LANES:]
+        upper_re, upper_im = upper[:, :LANES], -upper[:, LANES:]
+        if block == 0:
+            first = lane_ids == 0
+            lower_im = jnp.where(first, 0.0, lower_im)
+            upper_re = jnp.where(first, evens[:, LANES:], upper_re)
+            upper_im = jnp.where(first, odds[:, LANES:], upper_im)
+        for place, real, imag in ((block, lower_re, lower_im), (block + BLOCKS // 2, upper_re, upper_im)):
+            spec[place, :, :LANES] = real
+            spec[place, :, LANES:] = imag
+            amp[:, pl.ds(place * LANES, LANES)] = jnp.sqrt(real * real + imag * imag).astype(BF16)
+
+    wide_ids = lax.broadcasted_iota(jnp.int32, (1, 2 * LANES), 1)
     for pair in range(BLOCKS // 2):
-        parity, place = divmod(pair, 2)
         total = None
-        for other in range(4):
-            near = jnp.dot(
-                amp[:, pl.ds(other * 2 * LANES, 2 * LANES)],
-                bands[other // 2 - parity, other % 2 - place],
-                preferred_element_type=F32,
-            )
-            total = near if total is None else total + near
-        bin_ids = 2 * (lane_ids + place * 2 * LANES) + parity
+        for other in range(BLOCKS // 2):
+            if (other, pair) in bands:
+                near = jnp.dot(
+                    amp[:, pl.ds(other * 2 * LANES, 2 * LANES)],
+                    bands[other, pair],
+                    preferred_element_type=F32,
+                )
+                total = near if total is None else total + near
+        bin_ids = wide_ids + (pair % 2) * 2 * LANES
+        if pair >= 2:
+            bin_ids = jnp.where(bin_ids == 0, BINS // 2, BINS - bin_ids)
         count = jnp.minimum(bin_ids, SMOOTH) + jnp.minimum(BINS - 1 - bin_ids, SMOOTH) + 1
         scale = 1.0 / (total * (1.0 / count.astype(F32)) + 1e-6)
         for half in range(2):
@@ -158,30 +198,43 @@
 
 
 def whiten_kernel(
-    own_ref, pair_ref, next1_ref, next2_ref, next3_ref, even_table, odd_hbm,
-    spec, send, flags, odd_table, even, odd, amp, sem,
+    own_ref, pair_ref, next1_ref, next2_ref, next3_ref, early_table, late_hbm, inverse_hbm,
+    spec, send, flags, inverse, late_table, even, odd, amp, sems,
 ):
-    odd_copy = pltpu.make_async_copy(odd_hbm, odd_table, sem)
-    odd_copy.start()
+    late_copies = [
+        pltpu.make_async_copy(late_hbm.at[part], late_table.at[part], sems.at[part])
+        for part in range(BLOCKS - EARLY)
+    ]
+    for copy in late_copies:
+        copy.start()
+    inverse_copy = pltpu.make_async_copy(inverse_hbm, inverse, sems.at[BLOCKS - EARLY])
+    inverse_copy.start()
     line = lax.axis_index("y")
     side = lax.axis_index("zh")
-    store_sources(own_ref, even, odd)
+    for part in range(SLICES // 2):
+        lanes = pl.ds(part * LANES, LANES)
+        even[pl.ds(0, HELD), lanes] = unmark(own_ref[2 * part].reshape(HELD, LANES))
+        odd[pl.ds(0, HELD), lanes] = unmark(own_ref[2 * part + 1].reshape(HELD, LANES))
     for step, ref in enumerate((pair_ref, next1_ref, next2_ref, next3_ref)):
         for swap in range(2):
-            win = lax.rem(line + 4 - step, 4) * 2 + lax.rem(side + swap, 2)
+            win = lax.rem(line + step, 4) * 2 + lax.rem(side + swap, 2)
             first = pl.multiple_of(win * OWN, OWN)
+            where = pl.ds(HELD + first, OWN)
             received = ref[swap * OWN : swap * OWN + OWN, :]
-            where = pl.ds(HELD + first, OWN)
-            store_folded(even, odd, where, slice(None), received[:, :FOLD], received[:, FOLD:])
+            for part in range(SLICES // 2):
+                lanes, start = pl.ds(part * LANES, LANES), 2 * part * LANES
+                even[where, lanes] = unmark(received[:, start : start + LANES])
+                odd[where, lanes] = unmark(received[:, start + LANES : start + 2 * LANES])
             flags[pl.ds(first, OWN), :] = usable_lanes(received[:, :LANES])
-    whiten(even, odd, even_table, odd_table, spec, amp, odd_copy.wait)
+    whiten(even, odd, early_table, late_table, late_copies, spec, amp)
     send[:BLOCKS] = spec[:, :HELD, :].astype(BF16)
     usable = usable_lanes(own_ref[0].reshape(HELD, LANES)).astype(BF16)
     send[BLOCKS, :, :LANES] = usable
     send[BLOCKS, :, LANES:] = usable
-
-
-def correlate(sources, flags, ready, rec_flags, inverse, store, held, added, cross, before_inverse):
+    inverse_copy.wait()
+
+
+def correlate(sources, flags, ready, rec_flags, inverse, store, held, added, cross):
     held[...] = sources[:BLOCKS].astype(F32)
     added[...] = held[:, :, :LANES] + held[:, :, LANES:]
 
@@ -207,7 +260,6 @@
         return carry
 
     lax.fori_loop(0, BLOCKS, one_block, 0)
-    before_inverse()
     lagged = jnp.dot(cross[0], inverse[0], preferred_element_type=F32)
     for block in range(1, BLOCKS):
         lagged += jnp.dot(cross[block], inverse[block], preferred_element_type=F32)
@@ -223,15 +275,12 @@
             store(index, lanes, (lagged[index * OWN : index * OWN + OWN, lanes] * scale).astype(BF16))
 
 
-def own_kernel(send, ready, rec_flags, inverse_hbm, own_lags, inverse, held, added, cross, sem):
-    inverse_copy = pltpu.make_async_copy(inverse_hbm, inverse, sem)
-    inverse_copy.start()
-
+def own_kernel(send, ready, rec_flags, inverse, own_lags, held, added, cross):
     def store(index, lanes, values):
         own_lags[index, :, lanes] = values
 
     usable = send[BLOCKS, :, :LANES].astype(F32)
-    correlate(send, usable, ready, rec_flags, inverse, store, held, added, cross, inverse_copy.wait)
+    correlate(send, usable, ready, rec_flags, inverse, store, held, added, cross)
 
 
 def other_kernel(received, ready, rec_flags, inverse, own_lags, out_ref, held, added, cross):
@@ -242,7 +291,7 @@
         out_ref[(1 - core) * 8 + index, :, lanes] = values
 
     usable = received[BLOCKS, :, :LANES].astype(F32)
-    correlate(received, usable, ready, rec_flags, inverse, store, held, added, cross, lambda: None)
+    correlate(received, usable, ready, rec_flags, inverse, store, held, added, cross)
 
 
 def in_vmem(value):
@@ -260,7 +309,9 @@
         out_specs=[VMEM_SPEC] * 2,
         out_shape=(pltpu.VMEM((2 * SLICES, OWN, LANES), BF16), pltpu.VMEM((OWN, LENGTH), BF16)),
     )(rows_in, usable.reshape(1, OWN))
-    all_channels = lax.all_to_all(slices, ("x", "z", "core"), 0, 0)
+    all_channels = lax.cond(
+        lax.axis_index("core") < 2, lambda v: lax.all_to_all(v, ("x", "z", "core"), 0, 0), lambda v: v, slices
+    )
     opposite = lax.ppermute(rows, "zh", [(0, 1), (1, 0)])
     picked, pair, token = pl.pallas_call(
         pick_kernel,
@@ -276,36 +327,38 @@
         load_kernel,
         in_specs=[VMEM_SPEC, HBM_SPEC],
         out_specs=VMEM_SPEC,
-        out_shape=pltpu.VMEM((BLOCKS // 2, FOLD, 2 * LANES), BF16),
+        out_shape=pltpu.VMEM((EARLY, FOLD, 2 * LANES), BF16),
         scratch_shapes=[pltpu.SemaphoreType.DMA(())],
         compiler_params=pltpu.CompilerParams(vmem_limit_bytes=2**20),
-    )(token, in_hbm(forward_table()[: BLOCKS // 2]))
-    nexts = [lax.ppermute(pair, "y", [(i, (i + k) % 4) for i in range(4)]) for k in (1, 2, 3)]
+    )(token, in_hbm(forward_table()[:EARLY]))
+    nexts = [lax.ppermute(pair, "y", [(i, (i - k) % 4) for i in range(4)]) for k in (1, 2, 3)]
     own = lax.all_to_all(picked, ("x", "z", "y", "zh"), 0, 0)
     own, nexts, table = lax.optimization_barrier((own, nexts, table))
     own = own.reshape(SLICES, WINS, 8, LANES)
     rows = HELD + WINS * OWN
     limit = pltpu.CompilerParams(vmem_limit_bytes=16 * 2**20)
-    ready, send, flags = pl.pallas_call(
+    ready, send, flags, inverse = pl.pallas_call(
         whiten_kernel,
-        in_specs=[VMEM_SPEC] * 6 + [HBM_SPEC],
-        out_specs=[VMEM_SPEC] * 3,
+        in_specs=[VMEM_SPEC] * 6 + [HBM_SPEC] * 2,
+        out_specs=[VMEM_SPEC] * 4,
         out_shape=(
             pltpu.VMEM((BLOCKS, rows, 2 * LANES), F32),
             pltpu.VMEM((BLOCKS + 1, HELD, 2 * LANES), BF16),
             pltpu.VMEM((WINS * OWN, LANES), F32),
+            pltpu.VMEM((BLOCKS, 2 * LANES, LAGS), BF16),
         ),
         scratch_shapes=[
-            pltpu.VMEM((BLOCKS // 2, FOLD, 2 * LANES), BF16),
+            pltpu.VMEM((BLOCKS - EARLY, FOLD, 2 * LANES), BF16),
             pltpu.VMEM((rows, FOLD), BF16),
             pltpu.VMEM((rows, FOLD), BF16),
             pltpu.VMEM((rows, BINS), BF16),
-            pltpu.SemaphoreType.DMA(()),
+            pltpu.SemaphoreType.DMA((BLOCKS - EARLY + 1,)),
         ],
         compiler_params=limit,
     )(
         *(in_vmem(value) for value in (own, pair, *nexts, table)),
-        in_hbm(forward_table()[BLOCKS // 2 :]),
+        in_hbm(forward_table()[EARLY:]),
+        in_hbm(inverse_table()),
     )
     received = lax.ppermute(send, "core", [(0, 1), (1, 0)])
     scratch = [
@@ -313,14 +366,14 @@
         pltpu.VMEM((BLOCKS, HELD, LANES), F32),
         pltpu.VMEM((BLOCKS, 8 * OWN, 2 * LANES), BF16),
     ]
-    own_lags, inverse = pl.pallas_call(
+    own_lags = pl.pallas_call(
         own_kernel,
-        in_specs=[VMEM_SPEC] * 3 + [HBM_SPEC],
-        out_specs=[VMEM_SPEC] * 2,
-        out_shape=(pltpu.VMEM((8, OWN, LAGS), BF16), pltpu.VMEM((BLOCKS, 2 * LANES, LAGS), BF16)),
-        scratch_shapes=[*scratch, pltpu.SemaphoreType.DMA(())],
+        in_specs=[VMEM_SPEC] * 4,
+        out_specs=VMEM_SPEC,
+        out_shape=pltpu.VMEM((8, OWN, LAGS), BF16),
+        scratch_shapes=scratch,
         compiler_params=limit,
-    )(*(in_vmem(value) for value in (send, ready, flags)), in_hbm(inverse_table()))
+    )(*(in_vmem(value) for value in (send, ready, flags, inverse)))
     return pl.pallas_call(
         other_kernel,
         out_shape=jax.ShapeDtypeStruct((OWN, OWN, LAGS), BF16),

time: 58.9 us -> 55.9 us (0.949)
  blocking collectives: 0 us -> 15.3 us
  starting transfers between devices: 32.5 us -> 22.9 us
  waiting for transfers between devices: 13.7 us -> 6.27 us
  Pallas kernels: 12.3 us -> 11.1 us
    all_to_all x0 -> x1, blocking collectives: none -> 15.3 us  [local(): lax.all_to_all(v, ('x', 'z', 'core'), 0, 0)]
    all_to_all x1 -> x0, starting transfers between devices: 10 us -> none  [local(): all_channels = lax.all_to_all(slices, ('x', 'z', 'core'), 0, 0)]
    all_to_all x1, starting transfers between devices: 13.5 us -> 7.71 us  [local(): own = lax.all_to_all(picked, ('x', 'z', 'y', 'zh'), 0, 0)]
    ppermute x1, waiting for transfers between devices: 4.47 us -> 0.01 us  [local(): opposite = lax.ppermute(rows, 'zh', [(0, 1), (1, 0)])]
    ppermute x3, waiting for transfers between devices: 9.22 us -> 5.04 us  [local(): lax.ppermute(pair, 'y', [(i, (i - k) % 4) for i in range(4)])]
    ppermute x1, starting transfers between devices: 4.3 us -> 7.81 us  [local(): opposite = lax.ppermute(rows, 'zh', [(0, 1), (1, 0)])]
    ppermute x1, starting transfers between devices: 1.59 us -> 3.17 us  [local(): received = lax.ppermute(send, 'core', [(0, 1), (1, 0)])]
    all_to_all x1, waiting for transfers between devices: 0.01 us -> 1.22 us  [local(): own = lax.all_to_all(picked, ('x', 'z', 'y', 'zh'), 0, 0)]
  transfers between devices with their start and end apart: 7 -> 6, of which waited for: 5 -> 3; matrix products, arithmetic and copies ran while one was open for 0% -> 0% of each run, Pallas kernels for 6% -> 6%
where the time goes in v3:
time: 55.9 us; the launch traced here: 55.6 us
  starting transfers between devices  22.9 us (41%)
  blocking collectives  15.3 us (27%)
  Pallas kernels  11.1 us (20%)
  waiting for transfers between devices  6.27 us (11%)
    all_to_all x1, blocking collectives, local(): lax.all_to_all(v, ('x', 'z', 'core'), 0, 0)  15.3 us
    ppermute x1, starting transfers between devices, local(): opposite = lax.ppermute(rows, 'zh', [(0, 1), (1, 0)])  7.81 us
    all_to_all x1, starting transfers between devices, local(): own = lax.all_to_all(picked, ('x', 'z', 'y', 'zh'), 0, 0)  7.71 us
    ppermute x3, waiting for transfers between devices, local(): lax.ppermute(pair, 'y', [(i, (i - k) % 4) for i in range(4)])  5.04 us
    ppermute x3, starting transfers between devices, local(): lax.ppermute(pair, 'y', [(i, (i - k) % 4) for i in range(4)])  4.23 us
    ppermute x1, starting transfers between devices, local(): received = lax.ppermute(send, 'core', [(0, 1), (1, 0)])  3.17 us
    pallas_call x1, Pallas kernels, local(): pl.pallas_call(whiten_kernel, in_specs=[VMEM_SPEC] * 6 + [HBM_SPEC] * 2,...  3.06 us
    pallas_call x1, Pallas kernels, local(): pl.pallas_call(other_kernel, out_shape=jax.ShapeDtypeStruct((OWN, OWN, LA...  2.12 us
  transfers between devices with their start and end apart: 6, of which 3 were waited for; matrix products, arithmetic and copies ran while one was open for 0% of the time, Pallas kernels for 6%

profile of v3, /device:TPU:1, one launch (start us, length us, event | category | flops | bytes accessed | tf_op | source)
XLA Modules:
  0.0 55.6 jit_solution(3818029657944806205)
XLA Ops:
  0.0 1.2 %shard_map.64 = (bf16[32,16,128]{2,1,0:T(8,128)(2,1)S(1)}, bf16[16,2048]{1,0:T(8,128)(2,1)S(1)}) custom-call(bf16[16,2048]{1,0:T(8,128)(2,1)} %bitcast.5, s32[1,16]{1,0:T(1,128)} %bitcast.6), custom_call_target="tpu_custom_call" | custom-call | tf_op jit(solution)/shard_map/pallas_call | solution.py:307
  1.2 7.8 %collective-permute-start = (bf16[16,2048]{1,0:T(8,128)(2,1)S(1)}, bf16[16,2048]{1,0:T(8,128)(2,1)S(1)}, u32[]{:S(2)}, u32[]{:S(2)}) collective-permute-start(bf16[16,2048]{1,0:T(8,128)(2,1)S(1)} %get-tuple-element.25.rows_ref), channel_id=1, source_target_pairs={{0,1},{1,0},{2,3},{3,2},{4,5},{5,4},{6,7},{7,6},{8,9},{9,8},{10,11... | collective-permute-start | bytes 196616 | tf_op jit(solution)/shard_map/ppermute | solution.py:315
  9.0 15.3 %conditional.1 = (bf16[32,16,128]{2,1,0:T(8,128)(2,1)S(1)}) conditional(s32[]{:T(128)} %convert_element_type.3, bf16[32,16,128]{2,1,0:T(8,128)(2,1)S(1)} %get-tuple-element.24, bf16[32,16,128]{2,1,0:T(8,128)(2,1)S(1)} %get-tuple-element.24), branch_computations={%region_0.0_spmd, %region_1.0_spmd} | conditional | bytes 524296 | solution.py:312
  9.0 15.3 %all_to_all.9 = bf16[32,16,128]{2,1,0:T(8,128)(2,1)S(1)} all-to-all(bf16[32,16,128]{2,1,0:T(8,128)(2,1)S(1)} %copy.9), channel_id=1, replica_groups=mesh['x'=4,'z'=4,'core'=2,'y'=4,'zh'=2] {'x','z','core'}, dimensions={0} | all-to-all | bytes 262144 | tf_op jit(solution)/shard_map/cond/branch_1_fun/all_to_all | solution.py:313
  24.3 0.0 collective-permute-done.opposite_ref
  24.3 1.6 %shard_map.65 = (bf16[128,8,128]{2,1,0:T(8,128)(2,1)}, bf16[32,2048]{1,0:T(8,128)(2,1)S(1)}, f32[8,128]{1,0:T(8,128)S(1)}) custom-call(s32[1,128]{1,0:T(1,128)} %bitcast.7, bf16[32,16,128]{2,1,0:T(8,128)(2,1)S(1)} %get-tuple-element.38.all_ref, bf16[16,2048]{1,0:T(8,128)(2,1)S(1)} %get-tuple-element.25.rows_ref, ...), custom_call_target="tpu_custom_call" | custom-call | tf_op jit(solution)/shard_map/pallas_call | solution.py:316
  25.9 7.7 %all-to-all-start.1 = ((bf16[128,8,128]{2,1,0:T(8,128)(2,1)}), bf16[128,8,128]{2,1,0:T(8,128)(2,1)S(1)}, u32[]{:S(2)}, u32[]{:S(2)}) async-start(bf16[128,8,128]{2,1,0:T(8,128)(2,1)} %get-tuple-element.26), calls=%async_computation.1 | async-start | bytes 524288 | tf_op jit(solution)/shard_map/all_to_all | solution.py:335
  33.6 0.7 %collective-permute-start.3 = (bf16[32,2048]{1,0:T(8,128)(2,1)S(1)}, bf16[32,2048]{1,0:T(8,128)(2,1)S(1)}, u32[]{:S(2)}, u32[]{:S(2)}) collective-permute-start(bf16[32,2048]{1,0:T(8,128)(2,1)S(1)} %get-tuple-element.27.pair_ref), channel_id=1, source_target_pairs={{0,2},{2,4},{4,6},{6,0},{1,3},{3,5},{5,7},{7,1},{8,10},{10,12},{12... | collective-permute-start | bytes 393224 | tf_op jit(solution)/shard_map/ppermute | solution.py:334
  34.3 2.4 %collective-permute-start.2 = (bf16[32,2048]{1,0:T(8,128)(2,1)S(1)}, bf16[32,2048]{1,0:T(8,128)(2,1)S(1)}, u32[]{:S(2)}, u32[]{:S(2)}) collective-permute-start(bf16[32,2048]{1,0:T(8,128)(2,1)S(1)} %get-tuple-element.27.pair_ref), channel_id=1, source_target_pairs={{0,4},{2,6},{4,0},{6,2},{1,5},{3,7},{5,1},{7,3},{8,12},{10,14},{12... | collective-permute-start | bytes 393224 | tf_op jit(solution)/shard_map/ppermute | solution.py:334
  36.6 1.2 %collective-permute-start.1 = (bf16[32,2048]{1,0:T(8,128)(2,1)S(1)}, bf16[32,2048]{1,0:T(8,128)(2,1)S(1)}, u32[]{:S(2)}, u32[]{:S(2)}) collective-permute-start(bf16[32,2048]{1,0:T(8,128)(2,1)S(1)} %get-tuple-element.27.pair_ref), channel_id=1, source_target_pairs={{0,6},{2,0},{4,2},{6,4},{1,7},{3,1},{5,3},{7,5},{8,14},{10,8},{12,... | collective-permute-start | bytes 393224 | tf_op jit(solution)/shard_map/ppermute | solution.py:334
  37.8 1.7 %shard_map.66.early_table = bf16[5,1024,256]{2,1,0:T(8,128)(2,1)S(1)} custom-call(f32[8,128]{1,0:T(8,128)S(1)} %get-tuple-element.28.token_ref, bf16[5,1024,256]{2,1,0:T(8,128)(2,1)} %constant.14.clone.table_hbm), custom_call_target="tpu_custom_call" | custom-call | tf_op jit(solution)/shard_map/pallas_call | solution.py:326
  39.6 0.0 collective-permute-done.3.next3_ref
  39.6 4.3 %collective-permute-done.2.next2_ref = bf16[32,2048]{1,0:T(8,128)(2,1)S(1)} collective-permute-done((bf16[32,2048]{1,0:T(8,128)(2,1)S(1)}, bf16[32,2048]{1,0:T(8,128)(2,1)S(1)}, u32[]{:S(2)}, u32[]{:S(2)}) %collective-permute-start.2) | collective-permute-done | bytes 131104 | tf_op jit(solution)/shard_map/ppermute | solution.py:334
  43.9 0.7 %collective-permute-done.1.next1_ref = bf16[32,2048]{1,0:T(8,128)(2,1)S(1)} collective-permute-done((bf16[32,2048]{1,0:T(8,128)(2,1)S(1)}, bf16[32,2048]{1,0:T(8,128)(2,1)S(1)}, u32[]{:S(2)}, u32[]{:S(2)}) %collective-permute-start.1) | collective-permute-done | bytes 131104 | tf_op jit(solution)/shard_map/ppermute | solution.py:334
  44.6 1.2 %all-to-all-done.1 = bf16[128,8,128]{2,1,0:T(8,128)(2,1)S(1)} async-done(((bf16[128,8,128]{2,1,0:T(8,128)(2,1)}), bf16[128,8,128]{2,1,0:T(8,128)(2,1)S(1)}, u32[]{:S(2)}, u32[]{:S(2)}) %all-to-all-start.1) | async-done | bytes 262176 | tf_op jit(solution)/shard_map/all_to_all | solution.py:335
  45.9 3.1 %shard_map.67 = (f32[8,192,256]{2,1,0:T(8,128)S(1)}, bf16[9,64,256]{2,1,0:T(8,128)(2,1)S(1)}, f32[128,128]{1,0:T(8,128)S(1)}, bf16[8,256,512]{2,1,0:T(8,128)(2,1)S(1)}) custom-call(bf16[16,8,8,128]{3,2,1,0:T(8,128)(2,1)S(1)} %bitcast.4, bf16[32,2048]{1,0:T(8,128)(2,1)S(1)} %get-tuple-element.27.pair_ref, ...), custom_call_target="tpu_custom_call" | custom-call | tf_op jit(solution)/shard_map/pallas_call | solution.py:340
  48.9 3.2 %collective-permute-start.4 = (bf16[9,64,256]{2,1,0:T(8,128)(2,1)S(1)}, bf16[9,64,256]{2,1,0:T(8,128)(2,1)S(1)}, u32[]{:S(2)}, u32[]{:S(2)}) collective-permute-start(bf16[9,64,256]{2,1,0:T(8,128)(2,1)S(1)} %get-tuple-element.34.send), channel_id=1, source_target_pairs={{0,8},{8,0},{1,9},{9,1},{2,10},{10,2},{3,11},{11,3},{4,12},{12,4},... | collective-permute-start | bytes 884744 | tf_op jit(solution)/shard_map/ppermute | solution.py:363
  52.1 1.4 %shard_map.68.own_lags = bf16[8,16,512]{2,1,0:T(8,128)(2,1)S(1)} custom-call(bf16[9,64,256]{2,1,0:T(8,128)(2,1)S(1)} %get-tuple-element.34.send, f32[8,192,256]{2,1,0:T(8,128)S(1)} %get-tuple-element.35.ready, f32[128,128]{1,0:T(8,128)S(1)} %get-tuple-element.36.rec_flags, bf16[8,256,512]{2,1,0:T(8,128)(2,1)S(1)} %get-tuple-element.37.inverse), custom_call_target="tpu_custom_call" | custom-call | tf_op jit(solution)/shard_map/pallas_call | solution.py:369
  53.5 0.0 collective-permute-done.4.received
  53.5 2.1 %shard_map.69 = bf16[16,16,512]{2,1,0:T(8,128)(2,1)} custom-call(bf16[9,64,256]{2,1,0:T(8,128)(2,1)S(1)} %collective-permute-done.4.received, f32[8,192,256]{2,1,0:T(8,128)S(1)} %get-tuple-element.35.ready, f32[128,128]{1,0:T(8,128)S(1)} %get-tuple-element.36.rec_flags, bf16[8,256,512]{2,1,0:T(8,128)(2,1)S(1)} %get-tuple-element.37.inverse, ...), custom_call_target="tpu_custom_call" | custom-call | tf_op jit(solution)/shard_map/pallas_call | solution.py:377
  (1 shorter events, 0.0 us)
Async XLA Ops:
  1.2 23.1 %collective-permute-start = (bf16[16,2048]{1,0:T(8,128)(2,1)S(1)}, bf16[16,2048]{1,0:T(8,128)(2,1)S(1)}, u32[]{:S(2)}, u32[]{:S(2)}) collective-permute-start(bf16[16,2048]{1,0:T(8,128)(2,1)S(1)} %get-tuple-element.25.rows_ref), channel_id=1, source_target_pairs={{0,1},{1,0},{2,3},{3,2},{4,5},{5,4},{6,7},{7,6},{8,9},{9,8},{10,11... | collective-permute-start | bytes 196616 | tf_op jit(solution)/shard_map/ppermute | solution.py:315
  25.9 20.0 %all-to-all-start.1 = ((bf16[128,8,128]{2,1,0:T(8,128)(2,1)}), bf16[128,8,128]{2,1,0:T(8,128)(2,1)S(1)}, u32[]{:S(2)}, u32[]{:S(2)}) async-start(bf16[128,8,128]{2,1,0:T(8,128)(2,1)} %get-tuple-element.26), calls=%async_computation.1 | async-start | bytes 524288 | tf_op jit(solution)/shard_map/all_to_all | solution.py:335
  33.6 6.0 %collective-permute-start.3 = (bf16[32,2048]{1,0:T(8,128)(2,1)S(1)}, bf16[32,2048]{1,0:T(8,128)(2,1)S(1)}, u32[]{:S(2)}, u32[]{:S(2)}) collective-permute-start(bf16[32,2048]{1,0:T(8,128)(2,1)S(1)} %get-tuple-element.27.pair_ref), channel_id=1, source_target_pairs={{0,2},{2,4},{4,6},{6,0},{1,3},{3,5},{5,7},{7,1},{8,10},{10,12},{12... | collective-permute-start | bytes 393224 | tf_op jit(solution)/shard_map/ppermute | solution.py:334
  34.3 9.7 %collective-permute-start.2 = (bf16[32,2048]{1,0:T(8,128)(2,1)S(1)}, bf16[32,2048]{1,0:T(8,128)(2,1)S(1)}, u32[]{:S(2)}, u32[]{:S(2)}) collective-permute-start(bf16[32,2048]{1,0:T(8,128)(2,1)S(1)} %get-tuple-element.27.pair_ref), channel_id=1, source_target_pairs={{0,4},{2,6},{4,0},{6,2},{1,5},{3,7},{5,1},{7,3},{8,12},{10,14},{12... | collective-permute-start | bytes 393224 | tf_op jit(solution)/shard_map/ppermute | solution.py:334
  36.6 8.0 %collective-permute-start.1 = (bf16[32,2048]{1,0:T(8,128)(2,1)S(1)}, bf16[32,2048]{1,0:T(8,128)(2,1)S(1)}, u32[]{:S(2)}, u32[]{:S(2)}) collective-permute-start(bf16[32,2048]{1,0:T(8,128)(2,1)S(1)} %get-tuple-element.27.pair_ref), channel_id=1, source_target_pairs={{0,6},{2,0},{4,2},{6,4},{1,7},{3,1},{5,3},{7,5},{8,14},{10,8},{12,... | collective-permute-start | bytes 393224 | tf_op jit(solution)/shard_map/ppermute | solution.py:334
  48.9 4.6 %collective-permute-start.4 = (bf16[9,64,256]{2,1,0:T(8,128)(2,1)S(1)}, bf16[9,64,256]{2,1,0:T(8,128)(2,1)S(1)}, u32[]{:S(2)}, u32[]{:S(2)}) collective-permute-start(bf16[9,64,256]{2,1,0:T(8,128)(2,1)S(1)} %get-tuple-element.34.send), channel_id=1, source_target_pairs={{0,8},{8,0},{1,9},{9,1},{2,10},{10,2},{3,11},{11,3},{4,12},{12,4},... | collective-permute-start | bytes 884744 | tf_op jit(solution)/shard_map/ppermute | solution.py:363

commit v4 on v3

--- a/solution.py
+++ b/solution.py
@@ -12,7 +12,6 @@
 
 LENGTH = 2048
 BINS = LENGTH // 2
-FOLD = LENGTH // 2
 HALF = 256
 LAGS = 2 * HALF
 SMOOTH = 32
@@ -24,7 +23,7 @@
 SOURCES = 128
 CHANNELS = 512
 HELD = WINS * 8
-EARLY = 5
+EIGHTH = 0.70703125
 MARK = 1e30
 MARK_LIMIT = 1e29
 BF16 = jnp.bfloat16
@@ -34,26 +33,20 @@
 
 
 def bin_order():
-    lower = np.arange(BINS // 2)
-    upper = BINS - lower
-    upper[0] = BINS // 2
-    return np.concatenate([lower, upper])
+    low = np.arange(BINS // 4)
+    order = np.stack([low, BINS // 2 - low, BINS // 2 + low, BINS - low])
+    order[1, 0], order[3, 0] = BINS // 4, 3 * BINS // 4
+    return order.reshape(-1)
 
 
 def forward_table():
-    samples = np.arange(LENGTH).reshape(FOLD, 2).T[:, :, None]
-    bins = np.arange(BINS // 2)[None, None, :]
-
-    def angle(product):
-        return (product % LENGTH).astype(np.float32) * np.float32(2.0 * math.pi / LENGTH)
-
-    phases = angle(samples * bins)
+    samples = np.arange(LENGTH).reshape(LENGTH // 4, 4).T[:, :, None]
+    bins = np.arange(BINS // 4)[None, None, :]
+    phases = (samples * bins % LENGTH).astype(np.float32) * np.float32(2.0 * math.pi / LENGTH)
     real, imag = np.cos(phases), -np.sin(phases)
-    middle = angle(samples[:, :, 0] * (BINS // 2))
-    imag[0, :, 0] = np.cos(middle[0])
-    imag[1, :, 0] = -np.sin(middle[1])
-    table = np.stack([real, imag], axis=2).reshape(2, FOLD, 2, BLOCKS // 2, LANES)
-    return table.transpose(3, 0, 1, 2, 4).reshape(BLOCKS, FOLD, 2 * LANES).astype(jnp.bfloat16)
+    imag[:, :, 0] = 1 - 2 * (np.arange(LENGTH // 4) % 2)
+    table = np.stack([real, imag], axis=2).reshape(4, LENGTH // 4, 2, 2, LANES)
+    return table.transpose(3, 0, 1, 2, 4).reshape(8, LENGTH // 4, 2 * LANES).astype(jnp.bfloat16)
 
 
 def inverse_table():
@@ -75,10 +68,10 @@
     flags = jnp.broadcast_to(usable_ref[...].astype(F32), (OWN, OWN))
     flag = jnp.sum(jnp.where(row_ids == col_ids, flags, 0.0), axis=1, keepdims=True)
     marked = jnp.where(flag > 0.5, centred, MARK).astype(BF16)
-    wide = 2 * LANES
+    wide = 4 * LANES
     from_ids = lax.broadcasted_iota(jnp.int32, (wide, wide), 0)
     to_ids = lax.broadcasted_iota(jnp.int32, (wide, wide), 1)
-    taken = jnp.where(to_ids < LANES, 2 * to_ids, 2 * (to_ids - LANES) + 1)
+    taken = 4 * lax.rem(to_ids, LANES) + lax.div(to_ids, LANES)
     move = (from_ids == taken).astype(F32).astype(BF16)
     marked = jnp.concatenate(
         [
@@ -126,107 +119,100 @@
     return (values.astype(F32) < MARK_LIMIT).astype(F32)
 
 
+def bins_of(group, slot):
+    if group % 2 == 0:
+        return slot + group * (BINS // 4)
+    return jnp.where(slot == 0, group * (BINS // 4), (group + 1) * (BINS // 4) - slot)
+
+
 def band_tiles():
     rows = lax.broadcasted_iota(jnp.int32, (2 * LANES, 2 * LANES), 0)
     cols = lax.broadcasted_iota(jnp.int32, (2 * LANES, 2 * LANES), 1)
-    low, last = 2 * LANES, 2 * LANES - SMOOTH
-
-    def tile(inside):
-        return inside.astype(F32).astype(BF16)
-
-    near = jnp.abs(rows - cols) <= SMOOTH
-    below = jnp.abs(rows - cols - low) <= SMOOTH
-    above = jnp.abs(rows - cols + low) <= SMOOTH
-    row_middle, col_middle = (rows == 0) & (cols >= last), (cols == 0) & (rows >= last)
-    alone = (rows == 0) == (cols == 0)
-    same = tile(near)
-    facing = tile(rows + cols >= 2 * low - SMOOTH)
-    return {
-        (0, 0): same, (0, 1): tile(below), (1, 0): tile(above), (1, 1): same,
-        (2, 2): tile(near & alone), (2, 3): tile(below | row_middle), (3, 2): tile(above | col_middle),
-        (3, 3): same, (1, 3): facing, (3, 1): facing, (1, 2): tile(col_middle), (2, 1): tile(row_middle),
-    }
-
-
-def whiten(even, odd, early_table, late_table, late_copies, spec, amp):
+    tiles = {}
+    for pair in ((0, 0), (1, 1), (0, 1), (1, 0), (1, 2), (2, 1)):
+        apart = jnp.abs(bins_of(pair[0], rows) - bins_of(pair[1], cols))
+        tiles[pair] = (apart <= SMOOTH).astype(F32).astype(BF16)
+    for pair in ((2, 2), (3, 3), (2, 3), (3, 2)):
+        tiles[pair] = tiles[pair[0] - 2, pair[1] - 2]
+    return tiles
+
+
+def whiten(classes, table, spec, amp):
     bands = band_tiles()
-    lane_ids = lax.broadcasted_iota(jnp.int32, (1, LANES), 1)
-
-    def table(place):
-        if place < EARLY:
-            return early_table[place]
-        late_copies[place - EARLY].wait()
-        return late_table[place - EARLY]
-
-    for block in range(BLOCKS // 2):
-        evens = jnp.dot(even[...], table(2 * block), preferred_element_type=F32)
-        odds = jnp.dot(odd[...], table(2 * block + 1), preferred_element_type=F32)
-        lower, upper = evens + odds, evens - odds
-        lower_re, lower_im = lower[:, :LANES], lower[:, LANES:]
-        upper_re, upper_im = upper[:, :LANES], -upper[:, LANES:]
+    first = lax.broadcasted_iota(jnp.int32, (1, LANES), 1) == 0
+    for block in range(2):
+        parts = [jnp.dot(classes[r], table[4 * block + r], preferred_element_type=F32) for r in range(4)]
+        real = [part[:, :LANES] for part in parts]
+        imag = [part[:, LANES:] for part in parts]
+        sum02_re, sum02_im, gap02_re, gap02_im = real[0] + real[2], imag[0] + imag[2], real[0] - real[2], imag[0] - imag[2]
+        sum13_re, sum13_im, gap13_re, gap13_im = real[1] + real[3], imag[1] + imag[3], real[1] - real[3], imag[1] - imag[3]
+        bins = [
+            (sum02_re + sum13_re, sum02_im + sum13_im),
+            (gap02_re - gap13_im, -gap02_im - gap13_re),
+            (gap02_re + gap13_im, gap02_im - gap13_re),
+            (sum02_re - sum13_re, sum13_im - sum02_im),
+        ]
         if block == 0:
-            first = lane_ids == 0
-            lower_im = jnp.where(first, 0.0, lower_im)
-            upper_re = jnp.where(first, evens[:, LANES:], upper_re)
-            upper_im = jnp.where(first, odds[:, LANES:], upper_im)
-        for place, real, imag in ((block, lower_re, lower_im), (block + BLOCKS // 2, upper_re, upper_im)):
-            spec[place, :, :LANES] = real
-            spec[place, :, LANES:] = imag
-            amp[:, pl.ds(place * LANES, LANES)] = jnp.sqrt(real * real + imag * imag).astype(BF16)
+            gap, both = EIGHTH * gap13_im, EIGHTH * sum13_im
+            special = [
+                (bins[0][0], jnp.zeros_like(gap)),
+                (imag[0] + gap, -imag[2] - both),
+                (gap02_re, -gap13_re),
+                (imag[0] - gap, imag[2] - both),
+            ]
+            bins = [
+                tuple(jnp.where(first, new, old) for new, old in zip(at_first, at_rest))
+                for at_first, at_rest in zip(special, bins)
+            ]
+        for group, (re, im) in enumerate(bins):
+            place = 2 * group + block
+            spec[place, :, :LANES] = re
+            spec[place, :, LANES:] = im
+            amp[:, pl.ds(place * LANES, LANES)] = jnp.sqrt(re * re + im * im).astype(BF16)
 
     wide_ids = lax.broadcasted_iota(jnp.int32, (1, 2 * LANES), 1)
-    for pair in range(BLOCKS // 2):
+    for group in range(4):
         total = None
-        for other in range(BLOCKS // 2):
-            if (other, pair) in bands:
+        for other in range(4):
+            if (other, group) in bands:
                 near = jnp.dot(
                     amp[:, pl.ds(other * 2 * LANES, 2 * LANES)],
-                    bands[other, pair],
+                    bands[other, group],
                     preferred_element_type=F32,
                 )
                 total = near if total is None else total + near
-        bin_ids = wide_ids + (pair % 2) * 2 * LANES
-        if pair >= 2:
-            bin_ids = jnp.where(bin_ids == 0, BINS // 2, BINS - bin_ids)
+        bin_ids = bins_of(group, wide_ids)
         count = jnp.minimum(bin_ids, SMOOTH) + jnp.minimum(BINS - 1 - bin_ids, SMOOTH) + 1
         scale = 1.0 / (total * (1.0 / count.astype(F32)) + 1e-6)
         for half in range(2):
-            block = 2 * pair + half
+            block = 2 * group + half
             piece = scale[:, half * LANES : (half + 1) * LANES]
             spec[block, :, :LANES] = spec[block, :, :LANES] * piece
             spec[block, :, LANES:] = spec[block, :, LANES:] * piece
 
 
 def whiten_kernel(
-    own_ref, pair_ref, next1_ref, next2_ref, next3_ref, early_table, late_hbm, inverse_hbm,
-    spec, send, flags, inverse, late_table, even, odd, amp, sems,
+    own_ref, pair_ref, next1_ref, next2_ref, next3_ref, table, inverse_hbm,
+    spec, send, flags, inverse, classes, amp, sem,
 ):
-    late_copies = [
-        pltpu.make_async_copy(late_hbm.at[part], late_table.at[part], sems.at[part])
-        for part in range(BLOCKS - EARLY)
-    ]
-    for copy in late_copies:
-        copy.start()
-    inverse_copy = pltpu.make_async_copy(inverse_hbm, inverse, sems.at[BLOCKS - EARLY])
+    inverse_copy = pltpu.make_async_copy(inverse_hbm, inverse, sem)
     inverse_copy.start()
     line = lax.axis_index("y")
     side = lax.axis_index("zh")
-    for part in range(SLICES // 2):
-        lanes = pl.ds(part * LANES, LANES)
-        even[pl.ds(0, HELD), lanes] = unmark(own_ref[2 * part].reshape(HELD, LANES))
-        odd[pl.ds(0, HELD), lanes] = unmark(own_ref[2 * part + 1].reshape(HELD, LANES))
+    for part in range(SLICES):
+        lanes = pl.ds(part // 4 * LANES, LANES)
+        classes[part % 4, pl.ds(0, HELD), lanes] = unmark(own_ref[part].reshape(HELD, LANES))
     for step, ref in enumerate((pair_ref, next1_ref, next2_ref, next3_ref)):
         for swap in range(2):
             win = lax.rem(line + step, 4) * 2 + lax.rem(side + swap, 2)
             first = pl.multiple_of(win * OWN, OWN)
             where = pl.ds(HELD + first, OWN)
             received = ref[swap * OWN : swap * OWN + OWN, :]
-            for part in range(SLICES // 2):
-                lanes, start = pl.ds(part * LANES, LANES), 2 * part * LANES
-                even[where, lanes] = unmark(received[:, start : start + LANES])
-                odd[where, lanes] = unmark(received[:, start + LANES : start + 2 * LANES])
+            for part in range(SLICES):
+                lanes = pl.ds(part // 4 * LANES, LANES)
+                classes[part % 4, where, lanes] = unmark(received[:, part * LANES : (part + 1) * LANES])
             flags[pl.ds(first, OWN), :] = usable_lanes(received[:, :LANES])
-    whiten(even, odd, early_table, late_table, late_copies, spec, amp)
+    whiten(classes, table, spec, amp)
     send[:BLOCKS] = spec[:, :HELD, :].astype(BF16)
     usable = usable_lanes(own_ref[0].reshape(HELD, LANES)).astype(BF16)
     send[BLOCKS, :, :LANES] = usable
@@ -327,10 +313,10 @@
         load_kernel,
         in_specs=[VMEM_SPEC, HBM_SPEC],
         out_specs=VMEM_SPEC,
-        out_shape=pltpu.VMEM((EARLY, FOLD, 2 * LANES), BF16),
+        out_shape=pltpu.VMEM((8, LENGTH // 4, 2 * LANES), BF16),
         scratch_shapes=[pltpu.SemaphoreType.DMA(())],
         compiler_params=pltpu.CompilerParams(vmem_limit_bytes=2**20),
-    )(token, in_hbm(forward_table()[:EARLY]))
+    )(token, in_hbm(forward_table()))
     nexts = [lax.ppermute(pair, "y", [(i, (i - k) % 4) for i in range(4)]) for k in (1, 2, 3)]
     own = lax.all_to_all(picked, ("x", "z", "y", "zh"), 0, 0)
     own, nexts, table = lax.optimization_barrier((own, nexts, table))
@@ -339,7 +325,7 @@
     limit = pltpu.CompilerParams(vmem_limit_bytes=16 * 2**20)
     ready, send, flags, inverse = pl.pallas_call(
         whiten_kernel,
-        in_specs=[VMEM_SPEC] * 6 + [HBM_SPEC] * 2,
+        in_specs=[VMEM_SPEC] * 6 + [HBM_SPEC],
         out_specs=[VMEM_SPEC] * 4,
         out_shape=(
             pltpu.VMEM((BLOCKS, rows, 2 * LANES), F32),
@@ -348,16 +334,13 @@
             pltpu.VMEM((BLOCKS, 2 * LANES, LAGS), BF16),
         ),
         scratch_shapes=[
-            pltpu.VMEM((BLOCKS - EARLY, FOLD, 2 * LANES), BF16),
-            pltpu.VMEM((rows, FOLD), BF16),
-            pltpu.VMEM((rows, FOLD), BF16),
+            pltpu.VMEM((4, rows, LENGTH // 4), BF16),
             pltpu.VMEM((rows, BINS), BF16),
-            pltpu.SemaphoreType.DMA((BLOCKS - EARLY + 1,)),
+            pltpu.SemaphoreType.DMA(()),
         ],
         compiler_params=limit,
     )(
         *(in_vmem(value) for value in (own, pair, *nexts, table)),
-        in_hbm(forward_table()[EARLY:]),
         in_hbm(inverse_table()),
     )
     received = lax.ppermute(send, "core", [(0, 1), (1, 0)])

time: 55.9 us -> 55.4 us (level)
  Pallas kernels: 11.1 us -> 10.4 us
    pallas_call x1, Pallas kernels: 3.06 us -> 2.38 us  [local(): pl.pallas_call(whiten_kernel, in_specs=[VMEM_SPEC] * 6 + [HBM_SPEC], out_...]
  transfers between devices with their start and end apart: 6 -> 6, of which waited for: 3 -> 4; matrix products, arithmetic and copies ran while one was open for 0% -> 0% of each run, Pallas kernels for 6% -> 5%
where the time goes in v4:
time: 55.4 us; the launch traced here: 55.1 us
  starting transfers between devices  22.9 us (41%)
  blocking collectives  15.3 us (28%)
  Pallas kernels  10.4 us (19%)
  waiting for transfers between devices  6.42 us (12%)
    all_to_all x1, blocking collectives, local(): lax.all_to_all(v, ('x', 'z', 'core'), 0, 0)  15.3 us
    ppermute x1, starting transfers between devices, local(): opposite = lax.ppermute(rows, 'zh', [(0, 1), (1, 0)])  7.78 us
    all_to_all x1, starting transfers between devices, local(): own = lax.all_to_all(picked, ('x', 'z', 'y', 'zh'), 0, 0)  7.71 us
    ppermute x3, waiting for transfers between devices, local(): lax.ppermute(pair, 'y', [(i, (i - k) % 4) for i in range(4)])  5.2 us
    ppermute x3, starting transfers between devices, local(): lax.ppermute(pair, 'y', [(i, (i - k) % 4) for i in range(4)])  4.23 us
    ppermute x1, starting transfers between devices, local(): received = lax.ppermute(send, 'core', [(0, 1), (1, 0)])  3.17 us
    pallas_call x1, Pallas kernels, local(): pl.pallas_call(whiten_kernel, in_specs=[VMEM_SPEC] * 6 + [HBM_SPEC], out_...  2.38 us
    pallas_call x1, Pallas kernels, local(): pl.pallas_call(other_kernel, out_shape=jax.ShapeDtypeStruct((OWN, OWN, LA...  2.12 us
  transfers between devices with their start and end apart: 6, of which 4 were waited for; matrix products, arithmetic and copies ran while one was open for 0% of the time, Pallas kernels for 5%

profile of v4, /device:TPU:1, one launch (start us, length us, event | category | flops | bytes accessed | tf_op | source)
XLA Modules:
  0.0 55.1 jit_solution(16633844323176858480)
XLA Ops:
  0.0 1.3 %shard_map.55 = (bf16[32,16,128]{2,1,0:T(8,128)(2,1)S(1)}, bf16[16,2048]{1,0:T(8,128)(2,1)S(1)}) custom-call(bf16[16,2048]{1,0:T(8,128)(2,1)} %bitcast.5, s32[1,16]{1,0:T(1,128)} %bitcast.6), custom_call_target="tpu_custom_call" | custom-call | tf_op jit(solution)/shard_map/pallas_call | solution.py:293
  1.3 7.8 %collective-permute-start = (bf16[16,2048]{1,0:T(8,128)(2,1)S(1)}, bf16[16,2048]{1,0:T(8,128)(2,1)S(1)}, u32[]{:S(2)}, u32[]{:S(2)}) collective-permute-start(bf16[16,2048]{1,0:T(8,128)(2,1)S(1)} %get-tuple-element.25.rows_ref), channel_id=1, source_target_pairs={{0,1},{1,0},{2,3},{3,2},{4,5},{5,4},{6,7},{7,6},{8,9},{9,8},{10,11... | collective-permute-start | bytes 196616 | tf_op jit(solution)/shard_map/ppermute | solution.py:301
  9.1 15.3 %conditional.1 = (bf16[32,16,128]{2,1,0:T(8,128)(2,1)S(1)}) conditional(s32[]{:T(128)} %convert_element_type.3, bf16[32,16,128]{2,1,0:T(8,128)(2,1)S(1)} %get-tuple-element.24, bf16[32,16,128]{2,1,0:T(8,128)(2,1)S(1)} %get-tuple-element.24), branch_computations={%region_0.0_spmd, %region_1.0_spmd} | conditional | bytes 524296 | solution.py:298
  9.1 15.3 %all_to_all.9 = bf16[32,16,128]{2,1,0:T(8,128)(2,1)S(1)} all-to-all(bf16[32,16,128]{2,1,0:T(8,128)(2,1)S(1)} %copy.8), channel_id=1, replica_groups=mesh['x'=4,'z'=4,'core'=2,'y'=4,'zh'=2] {'x','z','core'}, dimensions={0} | all-to-all | bytes 262144 | tf_op jit(solution)/shard_map/cond/branch_1_fun/all_to_all | solution.py:299
  24.4 0.0 collective-permute-done.opposite_ref
  24.4 1.6 %shard_map.56 = (bf16[128,8,128]{2,1,0:T(8,128)(2,1)}, bf16[32,2048]{1,0:T(8,128)(2,1)S(1)}, f32[8,128]{1,0:T(8,128)S(1)}) custom-call(s32[1,128]{1,0:T(1,128)} %bitcast.7, bf16[32,16,128]{2,1,0:T(8,128)(2,1)S(1)} %get-tuple-element.38.all_ref, bf16[16,2048]{1,0:T(8,128)(2,1)S(1)} %get-tuple-element.25.rows_ref, ...), custom_call_target="tpu_custom_call" | custom-call | tf_op jit(solution)/shard_map/pallas_call | solution.py:302
  26.0 7.7 %all-to-all-start.1 = ((bf16[128,8,128]{2,1,0:T(8,128)(2,1)}), bf16[128,8,128]{2,1,0:T(8,128)(2,1)S(1)}, u32[]{:S(2)}, u32[]{:S(2)}) async-start(bf16[128,8,128]{2,1,0:T(8,128)(2,1)} %get-tuple-element.26), calls=%async_computation.1 | async-start | bytes 524288 | tf_op jit(solution)/shard_map/all_to_all | solution.py:321
  33.7 0.7 %collective-permute-start.3 = (bf16[32,2048]{1,0:T(8,128)(2,1)S(1)}, bf16[32,2048]{1,0:T(8,128)(2,1)S(1)}, u32[]{:S(2)}, u32[]{:S(2)}) collective-permute-start(bf16[32,2048]{1,0:T(8,128)(2,1)S(1)} %get-tuple-element.27.pair_ref), channel_id=1, source_target_pairs={{0,2},{2,4},{4,6},{6,0},{1,3},{3,5},{5,7},{7,1},{8,10},{10,12},{12... | collective-permute-start | bytes 393224 | tf_op jit(solution)/shard_map/ppermute | solution.py:320
  34.4 2.4 %collective-permute-start.2 = (bf16[32,2048]{1,0:T(8,128)(2,1)S(1)}, bf16[32,2048]{1,0:T(8,128)(2,1)S(1)}, u32[]{:S(2)}, u32[]{:S(2)}) collective-permute-start(bf16[32,2048]{1,0:T(8,128)(2,1)S(1)} %get-tuple-element.27.pair_ref), channel_id=1, source_target_pairs={{0,4},{2,6},{4,0},{6,2},{1,5},{3,7},{5,1},{7,3},{8,12},{10,14},{12... | collective-permute-start | bytes 393224 | tf_op jit(solution)/shard_map/ppermute | solution.py:320
  36.8 1.2 %collective-permute-start.1 = (bf16[32,2048]{1,0:T(8,128)(2,1)S(1)}, bf16[32,2048]{1,0:T(8,128)(2,1)S(1)}, u32[]{:S(2)}, u32[]{:S(2)}) collective-permute-start(bf16[32,2048]{1,0:T(8,128)(2,1)S(1)} %get-tuple-element.27.pair_ref), channel_id=1, source_target_pairs={{0,6},{2,0},{4,2},{6,4},{1,7},{3,1},{5,3},{7,5},{8,14},{10,8},{12,... | collective-permute-start | bytes 393224 | tf_op jit(solution)/shard_map/ppermute | solution.py:320
  38.0 1.6 %shard_map.57.table = bf16[8,512,256]{2,1,0:T(8,128)(2,1)S(1)} custom-call(f32[8,128]{1,0:T(8,128)S(1)} %get-tuple-element.28.token_ref, bf16[8,512,256]{2,1,0:T(8,128)(2,1)} %constant.12.clone.table_hbm), custom_call_target="tpu_custom_call" | custom-call | tf_op jit(solution)/shard_map/pallas_call | solution.py:312
  39.6 0.1 collective-permute-done.3.next3_ref
  39.7 4.4 %collective-permute-done.2.next2_ref = bf16[32,2048]{1,0:T(8,128)(2,1)S(1)} collective-permute-done((bf16[32,2048]{1,0:T(8,128)(2,1)S(1)}, bf16[32,2048]{1,0:T(8,128)(2,1)S(1)}, u32[]{:S(2)}, u32[]{:S(2)}) %collective-permute-start.2) | collective-permute-done | bytes 131104 | tf_op jit(solution)/shard_map/ppermute | solution.py:320
  44.0 0.7 %collective-permute-done.1.next1_ref = bf16[32,2048]{1,0:T(8,128)(2,1)S(1)} collective-permute-done((bf16[32,2048]{1,0:T(8,128)(2,1)S(1)}, bf16[32,2048]{1,0:T(8,128)(2,1)S(1)}, u32[]{:S(2)}, u32[]{:S(2)}) %collective-permute-start.1) | collective-permute-done | bytes 131104 | tf_op jit(solution)/shard_map/ppermute | solution.py:320
  44.8 1.2 %all-to-all-done.1 = bf16[128,8,128]{2,1,0:T(8,128)(2,1)S(1)} async-done(((bf16[128,8,128]{2,1,0:T(8,128)(2,1)}), bf16[128,8,128]{2,1,0:T(8,128)(2,1)S(1)}, u32[]{:S(2)}, u32[]{:S(2)}) %all-to-all-start.1) | async-done | bytes 262176 | tf_op jit(solution)/shard_map/all_to_all | solution.py:321
  46.0 2.4 %shard_map.58 = (f32[8,192,256]{2,1,0:T(8,128)S(1)}, bf16[9,64,256]{2,1,0:T(8,128)(2,1)S(1)}, f32[128,128]{1,0:T(8,128)S(1)}, bf16[8,256,512]{2,1,0:T(8,128)(2,1)S(1)}) custom-call(bf16[16,8,8,128]{3,2,1,0:T(8,128)(2,1)S(1)} %bitcast.4, bf16[32,2048]{1,0:T(8,128)(2,1)S(1)} %get-tuple-element.27.pair_ref, ...), custom_call_target="tpu_custom_call" | custom-call | tf_op jit(solution)/shard_map/pallas_call | solution.py:326
  48.4 3.2 %collective-permute-start.4 = (bf16[9,64,256]{2,1,0:T(8,128)(2,1)S(1)}, bf16[9,64,256]{2,1,0:T(8,128)(2,1)S(1)}, u32[]{:S(2)}, u32[]{:S(2)}) collective-permute-start(bf16[9,64,256]{2,1,0:T(8,128)(2,1)S(1)} %get-tuple-element.34.send), channel_id=1, source_target_pairs={{0,8},{8,0},{1,9},{9,1},{2,10},{10,2},{3,11},{11,3},{4,12},{12,4},... | collective-permute-start | bytes 884744 | tf_op jit(solution)/shard_map/ppermute | solution.py:346
  51.5 1.4 %shard_map.59.own_lags = bf16[8,16,512]{2,1,0:T(8,128)(2,1)S(1)} custom-call(bf16[9,64,256]{2,1,0:T(8,128)(2,1)S(1)} %get-tuple-element.34.send, f32[8,192,256]{2,1,0:T(8,128)S(1)} %get-tuple-element.35.ready, f32[128,128]{1,0:T(8,128)S(1)} %get-tuple-element.36.rec_flags, bf16[8,256,512]{2,1,0:T(8,128)(2,1)S(1)} %get-tuple-element.37.inverse), custom_call_target="tpu_custom_call" | custom-call | tf_op jit(solution)/shard_map/pallas_call | solution.py:352
  52.9 0.0 collective-permute-done.4.received
  52.9 2.1 %shard_map.60 = bf16[16,16,512]{2,1,0:T(8,128)(2,1)} custom-call(bf16[9,64,256]{2,1,0:T(8,128)(2,1)S(1)} %collective-permute-done.4.received, f32[8,192,256]{2,1,0:T(8,128)S(1)} %get-tuple-element.35.ready, f32[128,128]{1,0:T(8,128)S(1)} %get-tuple-element.36.rec_flags, bf16[8,256,512]{2,1,0:T(8,128)(2,1)S(1)} %get-tuple-element.37.inverse, ...), custom_call_target="tpu_custom_call" | custom-call | tf_op jit(solution)/shard_map/pallas_call | solution.py:360
  (1 shorter events, 0.0 us)
Async XLA Ops:
  1.3 23.1 %collective-permute-start = (bf16[16,2048]{1,0:T(8,128)(2,1)S(1)}, bf16[16,2048]{1,0:T(8,128)(2,1)S(1)}, u32[]{:S(2)}, u32[]{:S(2)}) collective-permute-start(bf16[16,2048]{1,0:T(8,128)(2,1)S(1)} %get-tuple-element.25.rows_ref), channel_id=1, source_target_pairs={{0,1},{1,0},{2,3},{3,2},{4,5},{5,4},{6,7},{7,6},{8,9},{9,8},{10,11... | collective-permute-start | bytes 196616 | tf_op jit(solution)/shard_map/ppermute | solution.py:301
  26.0 20.0 %all-to-all-start.1 = ((bf16[128,8,128]{2,1,0:T(8,128)(2,1)}), bf16[128,8,128]{2,1,0:T(8,128)(2,1)S(1)}, u32[]{:S(2)}, u32[]{:S(2)}) async-start(bf16[128,8,128]{2,1,0:T(8,128)(2,1)} %get-tuple-element.26), calls=%async_computation.1 | async-start | bytes 524288 | tf_op jit(solution)/shard_map/all_to_all | solution.py:321
  33.7 5.9 %collective-permute-start.3 = (bf16[32,2048]{1,0:T(8,128)(2,1)S(1)}, bf16[32,2048]{1,0:T(8,128)(2,1)S(1)}, u32[]{:S(2)}, u32[]{:S(2)}) collective-permute-start(bf16[32,2048]{1,0:T(8,128)(2,1)S(1)} %get-tuple-element.27.pair_ref), channel_id=1, source_target_pairs={{0,2},{2,4},{4,6},{6,0},{1,3},{3,5},{5,7},{7,1},{8,10},{10,12},{12... | collective-permute-start | bytes 393224 | tf_op jit(solution)/shard_map/ppermute | solution.py:320
  34.4 9.7 %collective-permute-start.2 = (bf16[32,2048]{1,0:T(8,128)(2,1)S(1)}, bf16[32,2048]{1,0:T(8,128)(2,1)S(1)}, u32[]{:S(2)}, u32[]{:S(2)}) collective-permute-start(bf16[32,2048]{1,0:T(8,128)(2,1)S(1)} %get-tuple-element.27.pair_ref), channel_id=1, source_target_pairs={{0,4},{2,6},{4,0},{6,2},{1,5},{3,7},{5,1},{7,3},{8,12},{10,14},{12... | collective-permute-start | bytes 393224 | tf_op jit(solution)/shard_map/ppermute | solution.py:320
  36.8 8.0 %collective-permute-start.1 = (bf16[32,2048]{1,0:T(8,128)(2,1)S(1)}, bf16[32,2048]{1,0:T(8,128)(2,1)S(1)}, u32[]{:S(2)}, u32[]{:S(2)}) collective-permute-start(bf16[32,2048]{1,0:T(8,128)(2,1)S(1)} %get-tuple-element.27.pair_ref), channel_id=1, source_target_pairs={{0,6},{2,0},{4,2},{6,4},{1,7},{3,1},{5,3},{7,5},{8,14},{10,8},{12,... | collective-permute-start | bytes 393224 | tf_op jit(solution)/shard_map/ppermute | solution.py:320
  48.4 4.6 %collective-permute-start.4 = (bf16[9,64,256]{2,1,0:T(8,128)(2,1)S(1)}, bf16[9,64,256]{2,1,0:T(8,128)(2,1)S(1)}, u32[]{:S(2)}, u32[]{:S(2)}) collective-permute-start(bf16[9,64,256]{2,1,0:T(8,128)(2,1)S(1)} %get-tuple-element.34.send), channel_id=1, source_target_pairs={{0,8},{8,0},{1,9},{9,1},{2,10},{10,2},{3,11},{11,3},{4,12},{12,4},... | collective-permute-start | bytes 884744 | tf_op jit(solution)/shard_map/ppermute | solution.py:346

commit v5 on v4

--- a/solution.py
+++ b/solution.py
@@ -92,31 +92,16 @@
     pair_ref[OWN:] = opposite_ref[...]
     core = lax.axis_index("core")
     rows = all_ref[...].reshape(CHANNELS, LANES)
-    channel_ids = lax.broadcasted_iota(jnp.int32, (CHANNELS, SOURCES), 0)
-    onehot = (channel_ids == sources_ref[...]).astype(F32).astype(BF16)
-    picked = lax.dot_general(
-        onehot, rows, (((0,), (0,)), ((), ())), preferred_element_type=F32
-    ).reshape(WINS, 2, 8, LANES)
-    half = jnp.where(core == 0, picked[:, 0], picked[:, 1]).astype(BF16)
+    row_ids = lax.broadcasted_iota(jnp.int32, (HELD, SOURCES), 0)
+    source_ids = lax.broadcasted_iota(jnp.int32, (HELD, SOURCES), 1)
+    here = source_ids == lax.div(row_ids, 8) * 16 + core * 8 + lax.rem(row_ids, 8)
+    wanted = jnp.sum(jnp.where(here, sources_ref[...].astype(F32), 0.0), axis=1, keepdims=True)
+    channel_ids = lax.broadcasted_iota(jnp.int32, (HELD, CHANNELS), 1)
+    onehot = (channel_ids == wanted.astype(jnp.int32)).astype(F32).astype(BF16)
+    half = jnp.dot(onehot, rows, preferred_element_type=F32).astype(BF16).reshape(WINS, 8, LANES)
     for place in range(SLICES):
         picked_ref[pl.ds(place * WINS, WINS)] = half
     token_ref[...] = jnp.zeros((8, LANES), F32)
-
-
-def load_kernel(token_ref, table_hbm, table_ref, sem):
-    del token_ref
-    copy = pltpu.make_async_copy(table_hbm, table_ref, sem)
-    copy.start()
-    copy.wait()
-
-
-def unmark(values):
-    widened = values.astype(F32)
-    return jnp.where(widened > MARK_LIMIT, 0.0, widened).astype(BF16)
-
-
-def usable_lanes(values):
-    return (values.astype(F32) < MARK_LIMIT).astype(F32)
 
 
 def bins_of(group, slot):
@@ -125,20 +110,36 @@
     return jnp.where(slot == 0, group * (BINS // 4), (group + 1) * (BINS // 4) - slot)
 
 
-def band_tiles():
+BANDS = ((0, 0), (1, 1), (0, 1), (1, 0), (1, 2))
+REPEATS = ((2, 2), (3, 3), (2, 3), (3, 2))
+
+
+def band_tile(pair):
     rows = lax.broadcasted_iota(jnp.int32, (2 * LANES, 2 * LANES), 0)
     cols = lax.broadcasted_iota(jnp.int32, (2 * LANES, 2 * LANES), 1)
-    tiles = {}
-    for pair in ((0, 0), (1, 1), (0, 1), (1, 0), (1, 2), (2, 1)):
-        apart = jnp.abs(bins_of(pair[0], rows) - bins_of(pair[1], cols))
-        tiles[pair] = (apart <= SMOOTH).astype(F32).astype(BF16)
-    for pair in ((2, 2), (3, 3), (2, 3), (3, 2)):
-        tiles[pair] = tiles[pair[0] - 2, pair[1] - 2]
-    return tiles
-
-
-def whiten(classes, table, spec, amp):
-    bands = band_tiles()
+    apart = jnp.abs(bins_of(pair[0], rows) - bins_of(pair[1], cols))
+    return (apart <= SMOOTH).astype(F32).astype(BF16)
+
+
+def load_kernel(token_ref, table_hbm, table_ref, bands_ref, sem):
+    del token_ref
+    copy = pltpu.make_async_copy(table_hbm, table_ref, sem)
+    copy.start()
+    for place, pair in enumerate(BANDS):
+        bands_ref[place] = band_tile(pair)
+    copy.wait()
+
+
+def unmark(values):
+    widened = values.astype(F32)
+    return jnp.where(widened > MARK_LIMIT, 0.0, widened).astype(BF16)
+
+
+def usable_lanes(values):
+    return (values.astype(F32) < MARK_LIMIT).astype(F32)
+
+
+def whiten(classes, table, bands, spec, amp):
     first = lax.broadcasted_iota(jnp.int32, (1, LANES), 1) == 0
     for block in range(2):
         parts = [jnp.dot(classes[r], table[4 * block + r], preferred_element_type=F32) for r in range(4)]
@@ -170,14 +171,17 @@
             spec[place, :, LANES:] = im
             amp[:, pl.ds(place * LANES, LANES)] = jnp.sqrt(re * re + im * im).astype(BF16)
 
+    tiles = {pair: bands[place] for place, pair in enumerate(BANDS)}
+    tiles.update({pair: bands[place] for place, pair in enumerate(REPEATS)})
+    tiles[2, 1] = band_tile((2, 1))
     wide_ids = lax.broadcasted_iota(jnp.int32, (1, 2 * LANES), 1)
     for group in range(4):
         total = None
         for other in range(4):
-            if (other, group) in bands:
+            if (other, group) in tiles:
                 near = jnp.dot(
                     amp[:, pl.ds(other * 2 * LANES, 2 * LANES)],
-                    bands[other, group],
+                    tiles[other, group],
                     preferred_element_type=F32,
                 )
                 total = near if total is None else total + near
@@ -192,7 +196,7 @@
 
 
 def whiten_kernel(
-    own_ref, pair_ref, next1_ref, next2_ref, next3_ref, table, inverse_hbm,
+    own_ref, pair_ref, next1_ref, next2_ref, next3_ref, table, bands, inverse_hbm,
     spec, send, flags, inverse, classes, amp, sem,
 ):
     inverse_copy = pltpu.make_async_copy(inverse_hbm, inverse, sem)
@@ -212,7 +216,7 @@
                 lanes = pl.ds(part // 4 * LANES, LANES)
                 classes[part % 4, where, lanes] = unmark(received[:, part * LANES : (part + 1) * LANES])
             flags[pl.ds(first, OWN), :] = usable_lanes(received[:, :LANES])
-    whiten(classes, table, spec, amp)
+    whiten(classes, table, bands, spec, amp)
     send[:BLOCKS] = spec[:, :HELD, :].astype(BF16)
     usable = usable_lanes(own_ref[0].reshape(HELD, LANES)).astype(BF16)
     send[BLOCKS, :, :LANES] = usable
@@ -309,23 +313,26 @@
             pltpu.VMEM((8, LANES), F32),
         ),
     )(sources.reshape(1, SOURCES), in_vmem(all_channels), in_vmem(rows), in_vmem(opposite))
-    table = pl.pallas_call(
+    table, bands = pl.pallas_call(
         load_kernel,
         in_specs=[VMEM_SPEC, HBM_SPEC],
-        out_specs=VMEM_SPEC,
-        out_shape=pltpu.VMEM((8, LENGTH // 4, 2 * LANES), BF16),
+        out_specs=[VMEM_SPEC] * 2,
+        out_shape=(
+            pltpu.VMEM((8, LENGTH // 4, 2 * LANES), BF16),
+            pltpu.VMEM((5, 2 * LANES, 2 * LANES), BF16),
+        ),
         scratch_shapes=[pltpu.SemaphoreType.DMA(())],
         compiler_params=pltpu.CompilerParams(vmem_limit_bytes=2**20),
     )(token, in_hbm(forward_table()))
     nexts = [lax.ppermute(pair, "y", [(i, (i - k) % 4) for i in range(4)]) for k in (1, 2, 3)]
     own = lax.all_to_all(picked, ("x", "z", "y", "zh"), 0, 0)
-    own, nexts, table = lax.optimization_barrier((own, nexts, table))
+    own, nexts, table, bands = lax.optimization_barrier((own, nexts, table, bands))
     own = own.reshape(SLICES, WINS, 8, LANES)
     rows = HELD + WINS * OWN
     limit = pltpu.CompilerParams(vmem_limit_bytes=16 * 2**20)
     ready, send, flags, inverse = pl.pallas_call(
         whiten_kernel,
-        in_specs=[VMEM_SPEC] * 6 + [HBM_SPEC],
+        in_specs=[VMEM_SPEC] * 7 + [HBM_SPEC],
         out_specs=[VMEM_SPEC] * 4,
         out_shape=(
             pltpu.VMEM((BLOCKS, rows, 2 * LANES), F32),
@@ -340,7 +347,7 @@
         ],
         compiler_params=limit,
     )(
-        *(in_vmem(value) for value in (own, pair, *nexts, table)),
+        *(in_vmem(value) for value in (own, pair, *nexts, table, bands)),
         in_hbm(inverse_table()),
     )
     received = lax.ppermute(send, "core", [(0, 1), (1, 0)])

time: 55.4 us -> 54.7 us (0.987)
  Pallas kernels: 10.4 us -> 9.78 us
    pallas_call x2, Pallas kernels: 3.97 us -> 3.34 us  [the longest x1 1.74 us: local(): pl.pallas_call(whiten_kernel, in_specs=[VMEM_SPEC] * 7 + [HBM_SPEC], out_...]
  transfers between devices with their start and end apart: 6 -> 6, of which waited for: 4 -> 4; matrix products, arithmetic and copies ran while one was open for 0% -> 0% of each run, Pallas kernels for 5% -> 6%
where the time goes in v5:
time: 54.7 us; the launch traced here: 54.4 us
  starting transfers between devices  22.9 us (42%)
  blocking collectives  15.3 us (28%)
  Pallas kernels  9.78 us (18%)
  waiting for transfers between devices  6.43 us (12%)
    all_to_all x1, blocking collectives, local(): lax.all_to_all(v, ('x', 'z', 'core'), 0, 0)  15.3 us
    ppermute x1, starting transfers between devices, local(): opposite = lax.ppermute(rows, 'zh', [(0, 1), (1, 0)])  7.78 us
    all_to_all x1, starting transfers between devices, local(): own = lax.all_to_all(picked, ('x', 'z', 'y', 'zh'), 0, 0)  7.71 us
    ppermute x3, waiting for transfers between devices, local(): lax.ppermute(pair, 'y', [(i, (i - k) % 4) for i in range(4)])  5.19 us
    ppermute x3, starting transfers between devices, local(): lax.ppermute(pair, 'y', [(i, (i - k) % 4) for i in range(4)])  4.23 us
    ppermute x1, starting transfers between devices, local(): received = lax.ppermute(send, 'core', [(0, 1), (1, 0)])  3.16 us
    pallas_call x1, Pallas kernels, local(): pl.pallas_call(other_kernel, out_shape=jax.ShapeDtypeStruct((OWN, OWN, LA...  2.13 us
    pallas_call x1, Pallas kernels, local(): pl.pallas_call(whiten_kernel, in_specs=[VMEM_SPEC] * 7 + [HBM_SPEC], out_...  1.74 us
  transfers between devices with their start and end apart: 6, of which 4 were waited for; matrix products, arithmetic and copies ran while one was open for 0% of the time, Pallas kernels for 6%

profile of v5, /device:TPU:1, one launch (start us, length us, event | category | flops | bytes accessed | tf_op | source)
XLA Modules:
  0.0 54.4 jit_solution(8948860639161946421)
XLA Ops:
  0.0 1.3 %shard_map.55 = (bf16[32,16,128]{2,1,0:T(8,128)(2,1)S(1)}, bf16[16,2048]{1,0:T(8,128)(2,1)S(1)}) custom-call(bf16[16,2048]{1,0:T(8,128)(2,1)} %bitcast.5, s32[1,16]{1,0:T(1,128)} %bitcast.6), custom_call_target="tpu_custom_call" | custom-call | tf_op jit(solution)/shard_map/pallas_call | solution.py:297
  1.3 7.8 %collective-permute-start = (bf16[16,2048]{1,0:T(8,128)(2,1)S(1)}, bf16[16,2048]{1,0:T(8,128)(2,1)S(1)}, u32[]{:S(2)}, u32[]{:S(2)}) collective-permute-start(bf16[16,2048]{1,0:T(8,128)(2,1)S(1)} %get-tuple-element.28.rows_ref), channel_id=1, source_target_pairs={{0,1},{1,0},{2,3},{3,2},{4,5},{5,4},{6,7},{7,6},{8,9},{9,8},{10,11... | collective-permute-start | bytes 196616 | tf_op jit(solution)/shard_map/ppermute | solution.py:305
  9.1 15.3 %conditional.1 = (bf16[32,16,128]{2,1,0:T(8,128)(2,1)S(1)}) conditional(s32[]{:T(128)} %convert_element_type.3, bf16[32,16,128]{2,1,0:T(8,128)(2,1)S(1)} %get-tuple-element.27, bf16[32,16,128]{2,1,0:T(8,128)(2,1)S(1)} %get-tuple-element.27), branch_computations={%region_0.0_spmd, %region_1.0_spmd} | conditional | bytes 524296 | solution.py:302
  9.1 15.3 %all_to_all.9 = bf16[32,16,128]{2,1,0:T(8,128)(2,1)S(1)} all-to-all(bf16[32,16,128]{2,1,0:T(8,128)(2,1)S(1)} %copy.8), channel_id=1, replica_groups=mesh['x'=4,'z'=4,'core'=2,'y'=4,'zh'=2] {'x','z','core'}, dimensions={0} | all-to-all | bytes 262144 | tf_op jit(solution)/shard_map/cond/branch_1_fun/all_to_all | solution.py:303
  24.4 0.0 collective-permute-done.opposite_ref
  24.4 1.6 %shard_map.56 = (bf16[128,8,128]{2,1,0:T(8,128)(2,1)}, bf16[32,2048]{1,0:T(8,128)(2,1)S(1)}, f32[8,128]{1,0:T(8,128)S(1)}) custom-call(s32[1,128]{1,0:T(1,128)} %bitcast.7, bf16[32,16,128]{2,1,0:T(8,128)(2,1)S(1)} %get-tuple-element.44.all_ref, bf16[16,2048]{1,0:T(8,128)(2,1)S(1)} %get-tuple-element.28.rows_ref, ...), custom_call_target="tpu_custom_call" | custom-call | tf_op jit(solution)/shard_map/pallas_call | solution.py:306
  26.0 7.7 %all-to-all-start.1 = ((bf16[128,8,128]{2,1,0:T(8,128)(2,1)}), bf16[128,8,128]{2,1,0:T(8,128)(2,1)S(1)}, u32[]{:S(2)}, u32[]{:S(2)}) async-start(bf16[128,8,128]{2,1,0:T(8,128)(2,1)} %get-tuple-element.29), calls=%async_computation.1 | async-start | bytes 524288 | tf_op jit(solution)/shard_map/all_to_all | solution.py:328
  33.7 0.7 %collective-permute-start.3 = (bf16[32,2048]{1,0:T(8,128)(2,1)S(1)}, bf16[32,2048]{1,0:T(8,128)(2,1)S(1)}, u32[]{:S(2)}, u32[]{:S(2)}) collective-permute-start(bf16[32,2048]{1,0:T(8,128)(2,1)S(1)} %get-tuple-element.30.pair_ref), channel_id=1, source_target_pairs={{0,2},{2,4},{4,6},{6,0},{1,3},{3,5},{5,7},{7,1},{8,10},{10,12},{12... | collective-permute-start | bytes 393224 | tf_op jit(solution)/shard_map/ppermute | solution.py:327
  34.4 2.4 %collective-permute-start.2 = (bf16[32,2048]{1,0:T(8,128)(2,1)S(1)}, bf16[32,2048]{1,0:T(8,128)(2,1)S(1)}, u32[]{:S(2)}, u32[]{:S(2)}) collective-permute-start(bf16[32,2048]{1,0:T(8,128)(2,1)S(1)} %get-tuple-element.30.pair_ref), channel_id=1, source_target_pairs={{0,4},{2,6},{4,0},{6,2},{1,5},{3,7},{5,1},{7,3},{8,12},{10,14},{12... | collective-permute-start | bytes 393224 | tf_op jit(solution)/shard_map/ppermute | solution.py:327
  36.8 1.2 %collective-permute-start.1 = (bf16[32,2048]{1,0:T(8,128)(2,1)S(1)}, bf16[32,2048]{1,0:T(8,128)(2,1)S(1)}, u32[]{:S(2)}, u32[]{:S(2)}) collective-permute-start(bf16[32,2048]{1,0:T(8,128)(2,1)S(1)} %get-tuple-element.30.pair_ref), channel_id=1, source_target_pairs={{0,6},{2,0},{4,2},{6,4},{1,7},{3,1},{5,3},{7,5},{8,14},{10,8},{12,... | collective-permute-start | bytes 393224 | tf_op jit(solution)/shard_map/ppermute | solution.py:327
  37.9 1.6 %shard_map.57 = (bf16[8,512,256]{2,1,0:T(8,128)(2,1)S(1)}, bf16[5,256,256]{2,1,0:T(8,128)(2,1)S(1)}) custom-call(f32[8,128]{1,0:T(8,128)S(1)} %get-tuple-element.31.token_ref, bf16[8,512,256]{2,1,0:T(8,128)(2,1)} %constant.12.clone.table_hbm), custom_call_target="tpu_custom_call" | custom-call | tf_op jit(solution)/shard_map/pallas_call | solution.py:316
  39.6 0.1 collective-permute-done.3.next3_ref
  39.6 4.4 %collective-permute-done.2.next2_ref = bf16[32,2048]{1,0:T(8,128)(2,1)S(1)} collective-permute-done((bf16[32,2048]{1,0:T(8,128)(2,1)S(1)}, bf16[32,2048]{1,0:T(8,128)(2,1)S(1)}, u32[]{:S(2)}, u32[]{:S(2)}) %collective-permute-start.2) | collective-permute-done | bytes 131104 | tf_op jit(solution)/shard_map/ppermute | solution.py:327
  44.0 0.7 %collective-permute-done.1.next1_ref = bf16[32,2048]{1,0:T(8,128)(2,1)S(1)} collective-permute-done((bf16[32,2048]{1,0:T(8,128)(2,1)S(1)}, bf16[32,2048]{1,0:T(8,128)(2,1)S(1)}, u32[]{:S(2)}, u32[]{:S(2)}) %collective-permute-start.1) | collective-permute-done | bytes 131104 | tf_op jit(solution)/shard_map/ppermute | solution.py:327
  44.7 1.2 %all-to-all-done.1 = bf16[128,8,128]{2,1,0:T(8,128)(2,1)S(1)} async-done(((bf16[128,8,128]{2,1,0:T(8,128)(2,1)}), bf16[128,8,128]{2,1,0:T(8,128)(2,1)S(1)}, u32[]{:S(2)}, u32[]{:S(2)}) %all-to-all-start.1) | async-done | bytes 262176 | tf_op jit(solution)/shard_map/all_to_all | solution.py:328
  46.0 1.7 %shard_map.58 = (f32[8,192,256]{2,1,0:T(8,128)S(1)}, bf16[9,64,256]{2,1,0:T(8,128)(2,1)S(1)}, f32[128,128]{1,0:T(8,128)S(1)}, bf16[8,256,512]{2,1,0:T(8,128)(2,1)S(1)}) custom-call(bf16[16,8,8,128]{3,2,1,0:T(8,128)(2,1)S(1)} %bitcast.4, bf16[32,2048]{1,0:T(8,128)(2,1)S(1)} %get-tuple-element.30.pair_ref, ...), custom_call_target="tpu_custom_call" | custom-call | tf_op jit(solution)/shard_map/pallas_call | solution.py:333
  47.7 3.2 %collective-permute-start.4 = (bf16[9,64,256]{2,1,0:T(8,128)(2,1)S(1)}, bf16[9,64,256]{2,1,0:T(8,128)(2,1)S(1)}, u32[]{:S(2)}, u32[]{:S(2)}) collective-permute-start(bf16[9,64,256]{2,1,0:T(8,128)(2,1)S(1)} %get-tuple-element.40.send), channel_id=1, source_target_pairs={{0,8},{8,0},{1,9},{9,1},{2,10},{10,2},{3,11},{11,3},{4,12},{12,4},... | collective-permute-start | bytes 884744 | tf_op jit(solution)/shard_map/ppermute | solution.py:353
  50.9 1.4 %shard_map.59.own_lags = bf16[8,16,512]{2,1,0:T(8,128)(2,1)S(1)} custom-call(bf16[9,64,256]{2,1,0:T(8,128)(2,1)S(1)} %get-tuple-element.40.send, f32[8,192,256]{2,1,0:T(8,128)S(1)} %get-tuple-element.41.ready, f32[128,128]{1,0:T(8,128)S(1)} %get-tuple-element.42.rec_flags, bf16[8,256,512]{2,1,0:T(8,128)(2,1)S(1)} %get-tuple-element.43.inverse), custom_call_target="tpu_custom_call" | custom-call | tf_op jit(solution)/shard_map/pallas_call | solution.py:359
  52.3 0.0 collective-permute-done.4.received
  52.3 2.1 %shard_map.60 = bf16[16,16,512]{2,1,0:T(8,128)(2,1)} custom-call(bf16[9,64,256]{2,1,0:T(8,128)(2,1)S(1)} %collective-permute-done.4.received, f32[8,192,256]{2,1,0:T(8,128)S(1)} %get-tuple-element.41.ready, f32[128,128]{1,0:T(8,128)S(1)} %get-tuple-element.42.rec_flags, bf16[8,256,512]{2,1,0:T(8,128)(2,1)S(1)} %get-tuple-element.43.inverse, ...), custom_call_target="tpu_custom_call" | custom-call | tf_op jit(solution)/shard_map/pallas_call | solution.py:367
  (1 shorter events, 0.0 us)
Async XLA Ops:
  1.3 23.1 %collective-permute-start = (bf16[16,2048]{1,0:T(8,128)(2,1)S(1)}, bf16[16,2048]{1,0:T(8,128)(2,1)S(1)}, u32[]{:S(2)}, u32[]{:S(2)}) collective-permute-start(bf16[16,2048]{1,0:T(8,128)(2,1)S(1)} %get-tuple-element.28.rows_ref), channel_id=1, source_target_pairs={{0,1},{1,0},{2,3},{3,2},{4,5},{5,4},{6,7},{7,6},{8,9},{9,8},{10,11... | collective-permute-start | bytes 196616 | tf_op jit(solution)/shard_map/ppermute | solution.py:305
  26.0 20.0 %all-to-all-start.1 = ((bf16[128,8,128]{2,1,0:T(8,128)(2,1)}), bf16[128,8,128]{2,1,0:T(8,128)(2,1)S(1)}, u32[]{:S(2)}, u32[]{:S(2)}) async-start(bf16[128,8,128]{2,1,0:T(8,128)(2,1)} %get-tuple-element.29), calls=%async_computation.1 | async-start | bytes 524288 | tf_op jit(solution)/shard_map/all_to_all | solution.py:328
  33.7 5.9 %collective-permute-start.3 = (bf16[32,2048]{1,0:T(8,128)(2,1)S(1)}, bf16[32,2048]{1,0:T(8,128)(2,1)S(1)}, u32[]{:S(2)}, u32[]{:S(2)}) collective-permute-start(bf16[32,2048]{1,0:T(8,128)(2,1)S(1)} %get-tuple-element.30.pair_ref), channel_id=1, source_target_pairs={{0,2},{2,4},{4,6},{6,0},{1,3},{3,5},{5,7},{7,1},{8,10},{10,12},{12... | collective-permute-start | bytes 393224 | tf_op jit(solution)/shard_map/ppermute | solution.py:327
  34.4 9.7 %collective-permute-start.2 = (bf16[32,2048]{1,0:T(8,128)(2,1)S(1)}, bf16[32,2048]{1,0:T(8,128)(2,1)S(1)}, u32[]{:S(2)}, u32[]{:S(2)}) collective-permute-start(bf16[32,2048]{1,0:T(8,128)(2,1)S(1)} %get-tuple-element.30.pair_ref), channel_id=1, source_target_pairs={{0,4},{2,6},{4,0},{6,2},{1,5},{3,7},{5,1},{7,3},{8,12},{10,14},{12... | collective-permute-start | bytes 393224 | tf_op jit(solution)/shard_map/ppermute | solution.py:327
  36.8 8.0 %collective-permute-start.1 = (bf16[32,2048]{1,0:T(8,128)(2,1)S(1)}, bf16[32,2048]{1,0:T(8,128)(2,1)S(1)}, u32[]{:S(2)}, u32[]{:S(2)}) collective-permute-start(bf16[32,2048]{1,0:T(8,128)(2,1)S(1)} %get-tuple-element.30.pair_ref), channel_id=1, source_target_pairs={{0,6},{2,0},{4,2},{6,4},{1,7},{3,1},{5,3},{7,5},{8,14},{10,8},{12,... | collective-permute-start | bytes 393224 | tf_op jit(solution)/shard_map/ppermute | solution.py:327
  47.7 4.6 %collective-permute-start.4 = (bf16[9,64,256]{2,1,0:T(8,128)(2,1)S(1)}, bf16[9,64,256]{2,1,0:T(8,128)(2,1)S(1)}, u32[]{:S(2)}, u32[]{:S(2)}) collective-permute-start(bf16[9,64,256]{2,1,0:T(8,128)(2,1)S(1)} %get-tuple-element.40.send), channel_id=1, source_target_pairs={{0,8},{8,0},{1,9},{9,1},{2,10},{10,2},{3,11},{11,3},{4,12},{12,4},... | collective-permute-start | bytes 884744 | tf_op jit(solution)/shard_map/ppermute | solution.py:353

commit v6 on v5

--- a/solution.py
+++ b/solution.py
@@ -249,7 +249,7 @@
                 cross[block, where, LANES:] = (sums[0] - sums[2]).astype(BF16)
         return carry
 
-    lax.fori_loop(0, BLOCKS, one_block, 0)
+    lax.fori_loop(0, BLOCKS, one_block, 0, unroll=True)
     lagged = jnp.dot(cross[0], inverse[0], preferred_element_type=F32)
     for block in range(1, BLOCKS):
         lagged += jnp.dot(cross[block], inverse[block], preferred_element_type=F32)

time: 54.7 us -> 54.2 us (level)
  Pallas kernels: 9.78 us -> 9.23 us
  transfers between devices with their start and end apart: 6 -> 6, of which waited for: 4 -> 5; matrix products, arithmetic and copies ran while one was open for 0% -> 0% of each run, Pallas kernels for 6% -> 5%
where the time goes in v6:
time: 54.2 us; the launch traced here: 53.9 us
  starting transfers between devices  22.9 us (42%)
  blocking collectives  15.3 us (28%)
  Pallas kernels  9.23 us (17%)
  waiting for transfers between devices  6.51 us (12%)
    all_to_all x1, blocking collectives, local(): lax.all_to_all(v, ('x', 'z', 'core'), 0, 0)  15.3 us
    ppermute x1, starting transfers between devices, local(): opposite = lax.ppermute(rows, 'zh', [(0, 1), (1, 0)])  7.78 us
    all_to_all x1, starting transfers between devices, local(): own = lax.all_to_all(picked, ('x', 'z', 'y', 'zh'), 0, 0)  7.71 us
    ppermute x3, waiting for transfers between devices, local(): lax.ppermute(pair, 'y', [(i, (i - k) % 4) for i in range(4)])  5.19 us
    ppermute x3, starting transfers between devices, local(): lax.ppermute(pair, 'y', [(i, (i - k) % 4) for i in range(4)])  4.23 us
    ppermute x1, starting transfers between devices, local(): received = lax.ppermute(send, 'core', [(0, 1), (1, 0)])  3.16 us
    pallas_call x1, Pallas kernels, local(): pl.pallas_call(other_kernel, out_shape=jax.ShapeDtypeStruct((OWN, OWN, LA...  1.84 us
    pallas_call x1, Pallas kernels, local(): pl.pallas_call(whiten_kernel, in_specs=[VMEM_SPEC] * 7 + [HBM_SPEC], out_...  1.74 us
  transfers between devices with their start and end apart: 6, of which 5 were waited for; matrix products, arithmetic and copies ran while one was open for 0% of the time, Pallas kernels for 5%

profile of v6, /device:TPU:1, one launch (start us, length us, event | category | flops | bytes accessed | tf_op | source)
XLA Modules:
  0.0 53.9 jit_solution(10207337230796905863)
XLA Ops:
  0.0 1.3 %shard_map.55 = (bf16[32,16,128]{2,1,0:T(8,128)(2,1)S(1)}, bf16[16,2048]{1,0:T(8,128)(2,1)S(1)}) custom-call(bf16[16,2048]{1,0:T(8,128)(2,1)} %bitcast.5, s32[1,16]{1,0:T(1,128)} %bitcast.6), custom_call_target="tpu_custom_call" | custom-call | tf_op jit(solution)/shard_map/pallas_call | solution.py:297
  1.3 7.8 %collective-permute-start = (bf16[16,2048]{1,0:T(8,128)(2,1)S(1)}, bf16[16,2048]{1,0:T(8,128)(2,1)S(1)}, u32[]{:S(2)}, u32[]{:S(2)}) collective-permute-start(bf16[16,2048]{1,0:T(8,128)(2,1)S(1)} %get-tuple-element.28.rows_ref), channel_id=1, source_target_pairs={{0,1},{1,0},{2,3},{3,2},{4,5},{5,4},{6,7},{7,6},{8,9},{9,8},{10,11... | collective-permute-start | bytes 196616 | tf_op jit(solution)/shard_map/ppermute | solution.py:305
  9.1 15.3 %conditional.1 = (bf16[32,16,128]{2,1,0:T(8,128)(2,1)S(1)}) conditional(s32[]{:T(128)} %convert_element_type.3, bf16[32,16,128]{2,1,0:T(8,128)(2,1)S(1)} %get-tuple-element.27, bf16[32,16,128]{2,1,0:T(8,128)(2,1)S(1)} %get-tuple-element.27), branch_computations={%region_0.0_spmd, %region_1.0_spmd} | conditional | bytes 524296 | solution.py:302
  9.1 15.3 %all_to_all.9 = bf16[32,16,128]{2,1,0:T(8,128)(2,1)S(1)} all-to-all(bf16[32,16,128]{2,1,0:T(8,128)(2,1)S(1)} %copy.8), channel_id=1, replica_groups=mesh['x'=4,'z'=4,'core'=2,'y'=4,'zh'=2] {'x','z','core'}, dimensions={0} | all-to-all | bytes 262144 | tf_op jit(solution)/shard_map/cond/branch_1_fun/all_to_all | solution.py:303
  24.4 0.0 collective-permute-done.opposite_ref
  24.4 1.6 %shard_map.56 = (bf16[128,8,128]{2,1,0:T(8,128)(2,1)}, bf16[32,2048]{1,0:T(8,128)(2,1)S(1)}, f32[8,128]{1,0:T(8,128)S(1)}) custom-call(s32[1,128]{1,0:T(1,128)} %bitcast.7, bf16[32,16,128]{2,1,0:T(8,128)(2,1)S(1)} %get-tuple-element.44.all_ref, bf16[16,2048]{1,0:T(8,128)(2,1)S(1)} %get-tuple-element.28.rows_ref, ...), custom_call_target="tpu_custom_call" | custom-call | tf_op jit(solution)/shard_map/pallas_call | solution.py:306
  26.0 7.7 %all-to-all-start.1 = ((bf16[128,8,128]{2,1,0:T(8,128)(2,1)}), bf16[128,8,128]{2,1,0:T(8,128)(2,1)S(1)}, u32[]{:S(2)}, u32[]{:S(2)}) async-start(bf16[128,8,128]{2,1,0:T(8,128)(2,1)} %get-tuple-element.29), calls=%async_computation.1 | async-start | bytes 524288 | tf_op jit(solution)/shard_map/all_to_all | solution.py:328
  33.7 0.7 %collective-permute-start.3 = (bf16[32,2048]{1,0:T(8,128)(2,1)S(1)}, bf16[32,2048]{1,0:T(8,128)(2,1)S(1)}, u32[]{:S(2)}, u32[]{:S(2)}) collective-permute-start(bf16[32,2048]{1,0:T(8,128)(2,1)S(1)} %get-tuple-element.30.pair_ref), channel_id=1, source_target_pairs={{0,2},{2,4},{4,6},{6,0},{1,3},{3,5},{5,7},{7,1},{8,10},{10,12},{12... | collective-permute-start | bytes 393224 | tf_op jit(solution)/shard_map/ppermute | solution.py:327
  34.4 2.4 %collective-permute-start.2 = (bf16[32,2048]{1,0:T(8,128)(2,1)S(1)}, bf16[32,2048]{1,0:T(8,128)(2,1)S(1)}, u32[]{:S(2)}, u32[]{:S(2)}) collective-permute-start(bf16[32,2048]{1,0:T(8,128)(2,1)S(1)} %get-tuple-element.30.pair_ref), channel_id=1, source_target_pairs={{0,4},{2,6},{4,0},{6,2},{1,5},{3,7},{5,1},{7,3},{8,12},{10,14},{12... | collective-permute-start | bytes 393224 | tf_op jit(solution)/shard_map/ppermute | solution.py:327
  36.8 1.2 %collective-permute-start.1 = (bf16[32,2048]{1,0:T(8,128)(2,1)S(1)}, bf16[32,2048]{1,0:T(8,128)(2,1)S(1)}, u32[]{:S(2)}, u32[]{:S(2)}) collective-permute-start(bf16[32,2048]{1,0:T(8,128)(2,1)S(1)} %get-tuple-element.30.pair_ref), channel_id=1, source_target_pairs={{0,6},{2,0},{4,2},{6,4},{1,7},{3,1},{5,3},{7,5},{8,14},{10,8},{12,... | collective-permute-start | bytes 393224 | tf_op jit(solution)/shard_map/ppermute | solution.py:327
  37.9 1.6 %shard_map.57 = (bf16[8,512,256]{2,1,0:T(8,128)(2,1)S(1)}, bf16[5,256,256]{2,1,0:T(8,128)(2,1)S(1)}) custom-call(f32[8,128]{1,0:T(8,128)S(1)} %get-tuple-element.31.token_ref, bf16[8,512,256]{2,1,0:T(8,128)(2,1)} %constant.12.clone.table_hbm), custom_call_target="tpu_custom_call" | custom-call | tf_op jit(solution)/shard_map/pallas_call | solution.py:316
  39.6 0.1 collective-permute-done.3.next3_ref
  39.6 4.4 %collective-permute-done.2.next2_ref = bf16[32,2048]{1,0:T(8,128)(2,1)S(1)} collective-permute-done((bf16[32,2048]{1,0:T(8,128)(2,1)S(1)}, bf16[32,2048]{1,0:T(8,128)(2,1)S(1)}, u32[]{:S(2)}, u32[]{:S(2)}) %collective-permute-start.2) | collective-permute-done | bytes 131104 | tf_op jit(solution)/shard_map/ppermute | solution.py:327
  44.0 0.7 %collective-permute-done.1.next1_ref = bf16[32,2048]{1,0:T(8,128)(2,1)S(1)} collective-permute-done((bf16[32,2048]{1,0:T(8,128)(2,1)S(1)}, bf16[32,2048]{1,0:T(8,128)(2,1)S(1)}, u32[]{:S(2)}, u32[]{:S(2)}) %collective-permute-start.1) | collective-permute-done | bytes 131104 | tf_op jit(solution)/shard_map/ppermute | solution.py:327
  44.7 1.2 %all-to-all-done.1 = bf16[128,8,128]{2,1,0:T(8,128)(2,1)S(1)} async-done(((bf16[128,8,128]{2,1,0:T(8,128)(2,1)}), bf16[128,8,128]{2,1,0:T(8,128)(2,1)S(1)}, u32[]{:S(2)}, u32[]{:S(2)}) %all-to-all-start.1) | async-done | bytes 262176 | tf_op jit(solution)/shard_map/all_to_all | solution.py:328
  46.0 1.7 %shard_map.58 = (f32[8,192,256]{2,1,0:T(8,128)S(1)}, bf16[9,64,256]{2,1,0:T(8,128)(2,1)S(1)}, f32[128,128]{1,0:T(8,128)S(1)}, bf16[8,256,512]{2,1,0:T(8,128)(2,1)S(1)}) custom-call(bf16[16,8,8,128]{3,2,1,0:T(8,128)(2,1)S(1)} %bitcast.4, bf16[32,2048]{1,0:T(8,128)(2,1)S(1)} %get-tuple-element.30.pair_ref, ...), custom_call_target="tpu_custom_call" | custom-call | tf_op jit(solution)/shard_map/pallas_call | solution.py:333
  47.7 3.2 %collective-permute-start.4 = (bf16[9,64,256]{2,1,0:T(8,128)(2,1)S(1)}, bf16[9,64,256]{2,1,0:T(8,128)(2,1)S(1)}, u32[]{:S(2)}, u32[]{:S(2)}) collective-permute-start(bf16[9,64,256]{2,1,0:T(8,128)(2,1)S(1)} %get-tuple-element.40.send), channel_id=1, source_target_pairs={{0,8},{8,0},{1,9},{9,1},{2,10},{10,2},{3,11},{11,3},{4,12},{12,4},... | collective-permute-start | bytes 884744 | tf_op jit(solution)/shard_map/ppermute | solution.py:353
  50.9 1.1 %shard_map.59.own_lags = bf16[8,16,512]{2,1,0:T(8,128)(2,1)S(1)} custom-call(bf16[9,64,256]{2,1,0:T(8,128)(2,1)S(1)} %get-tuple-element.40.send, f32[8,192,256]{2,1,0:T(8,128)S(1)} %get-tuple-element.41.ready, f32[128,128]{1,0:T(8,128)S(1)} %get-tuple-element.42.rec_flags, bf16[8,256,512]{2,1,0:T(8,128)(2,1)S(1)} %get-tuple-element.43.inverse), custom_call_target="tpu_custom_call" | custom-call | tf_op jit(solution)/shard_map/pallas_call | solution.py:359
  52.0 0.1 collective-permute-done.4.received
  52.1 1.8 %shard_map.60 = bf16[16,16,512]{2,1,0:T(8,128)(2,1)} custom-call(bf16[9,64,256]{2,1,0:T(8,128)(2,1)S(1)} %collective-permute-done.4.received, f32[8,192,256]{2,1,0:T(8,128)S(1)} %get-tuple-element.41.ready, f32[128,128]{1,0:T(8,128)S(1)} %get-tuple-element.42.rec_flags, bf16[8,256,512]{2,1,0:T(8,128)(2,1)S(1)} %get-tuple-element.43.inverse, ...), custom_call_target="tpu_custom_call" | custom-call | tf_op jit(solution)/shard_map/pallas_call | solution.py:367
  (1 shorter events, 0.0 us)
Async XLA Ops:
  1.3 23.1 %collective-permute-start = (bf16[16,2048]{1,0:T(8,128)(2,1)S(1)}, bf16[16,2048]{1,0:T(8,128)(2,1)S(1)}, u32[]{:S(2)}, u32[]{:S(2)}) collective-permute-start(bf16[16,2048]{1,0:T(8,128)(2,1)S(1)} %get-tuple-element.28.rows_ref), channel_id=1, source_target_pairs={{0,1},{1,0},{2,3},{3,2},{4,5},{5,4},{6,7},{7,6},{8,9},{9,8},{10,11... | collective-permute-start | bytes 196616 | tf_op jit(solution)/shard_map/ppermute | solution.py:305
  26.0 20.0 %all-to-all-start.1 = ((bf16[128,8,128]{2,1,0:T(8,128)(2,1)}), bf16[128,8,128]{2,1,0:T(8,128)(2,1)S(1)}, u32[]{:S(2)}, u32[]{:S(2)}) async-start(bf16[128,8,128]{2,1,0:T(8,128)(2,1)} %get-tuple-element.29), calls=%async_computation.1 | async-start | bytes 524288 | tf_op jit(solution)/shard_map/all_to_all | solution.py:328
  33.7 5.9 %collective-permute-start.3 = (bf16[32,2048]{1,0:T(8,128)(2,1)S(1)}, bf16[32,2048]{1,0:T(8,128)(2,1)S(1)}, u32[]{:S(2)}, u32[]{:S(2)}) collective-permute-start(bf16[32,2048]{1,0:T(8,128)(2,1)S(1)} %get-tuple-element.30.pair_ref), channel_id=1, source_target_pairs={{0,2},{2,4},{4,6},{6,0},{1,3},{3,5},{5,7},{7,1},{8,10},{10,12},{12... | collective-permute-start | bytes 393224 | tf_op jit(solution)/shard_map/ppermute | solution.py:327
  34.4 9.7 %collective-permute-start.2 = (bf16[32,2048]{1,0:T(8,128)(2,1)S(1)}, bf16[32,2048]{1,0:T(8,128)(2,1)S(1)}, u32[]{:S(2)}, u32[]{:S(2)}) collective-permute-start(bf16[32,2048]{1,0:T(8,128)(2,1)S(1)} %get-tuple-element.30.pair_ref), channel_id=1, source_target_pairs={{0,4},{2,6},{4,0},{6,2},{1,5},{3,7},{5,1},{7,3},{8,12},{10,14},{12... | collective-permute-start | bytes 393224 | tf_op jit(solution)/shard_map/ppermute | solution.py:327
  36.8 8.0 %collective-permute-start.1 = (bf16[32,2048]{1,0:T(8,128)(2,1)S(1)}, bf16[32,2048]{1,0:T(8,128)(2,1)S(1)}, u32[]{:S(2)}, u32[]{:S(2)}) collective-permute-start(bf16[32,2048]{1,0:T(8,128)(2,1)S(1)} %get-tuple-element.30.pair_ref), channel_id=1, source_target_pairs={{0,6},{2,0},{4,2},{6,4},{1,7},{3,1},{5,3},{7,5},{8,14},{10,8},{12,... | collective-permute-start | bytes 393224 | tf_op jit(solution)/shard_map/ppermute | solution.py:327
  47.7 4.4 %collective-permute-start.4 = (bf16[9,64,256]{2,1,0:T(8,128)(2,1)S(1)}, bf16[9,64,256]{2,1,0:T(8,128)(2,1)S(1)}, u32[]{:S(2)}, u32[]{:S(2)}) collective-permute-start(bf16[9,64,256]{2,1,0:T(8,128)(2,1)S(1)} %get-tuple-element.40.send), channel_id=1, source_target_pairs={{0,8},{8,0},{1,9},{9,1},{2,10},{10,2},{3,11},{11,3},{4,12},{12,4},... | collective-permute-start | bytes 884744 | tf_op jit(solution)/shard_map/ppermute | solution.py:353
